TPU v7x, 512 devices: a whole 4x4x16 slice. The times are simulated.
512 devices in a mesh: gx: 32 (over x, y, core), gy: 16 (over z).
Axes of the slice: x: 4, y: 4, z: 16, core: 2. Of those that a mesh axis runs over, the one named last changes fastest.
Arguments:
- right_side: float32 [2, 512, 2048], P(None, 'gx', 'gy'), may hold values from -160 to 160
- conductivity: float32 [512, 2048], P('gx', 'gy'), may hold values from 0.2 to 5
- leaf_inverse: float32 [128, 64, 128, 128], P('gx', 'gy'), may hold values from -1 to 4, as said below
- front_basis: float32 [512, 2048, 128], P('gx', 'gy'), may hold values from -0.25 to 0.25
- leaf_transfer: float32 [32, 16, 128, 128], P('gx', 'gy'), may hold values from -0.4375 to 0.4375
- node_transfer: float32 [32, 16, 8, 128, 128], P('gx', 'gy'), may hold values from -1 to 1, as said below
- leaf_front: float32 [32, 16, 128, 128], P('gx', 'gy'), may hold values from -1 to 1, as said below
- node_front: float32 [32, 16, 9, 128, 128], P('gx', 'gy'), may hold values from -1 to 1, as said below
Outputs:
- solution: float32 [2, 512, 2048], P(None, 'gx', 'gy')
- residual: float32 [2, 512, 2048], P(None, 'gx', 'gy')
- direction: float32 [2, 512, 2048], P(None, 'gx', 'gy')
Inputs may be any that keep to these rules, and one draw needn't show every extreme that they name: `leaf_inverse`: every block is symmetric and positive definite. `leaf_front`: every matrix is symmetric and positive definite. `node_front`: every matrix is symmetric and positive definite; entry h - 1 is the same for all tiles covered by one node of level h. `node_transfer`: entry h - 1 is the same for all tiles covered by one node of level h.
All inputs are finite; a program needn't handle non-finite values.
Results may differ from a plain program's by a relative error of at most 0.0001.
Values sent between devices are 32-bit elements; how exact they have to be, the bound alone decides.
A program may use at most 64 MiB of HBM per device.

v0:
```python
from functools import partial

import jax
import jax.numpy as jnp
from jax import lax
from jax.sharding import PartitionSpec as P

LBX = 4
LBY = 32


HIGHEST = lax.Precision.HIGHEST


def extended(cells, sides, width):
    for axis, dim in sides:
        count = lax.axis_size(axis)
        ends = count - 1
        head = lax.slice_in_dim(cells, 0, width, axis=dim)
        tail = lax.slice_in_dim(cells, cells.shape[dim] - width, cells.shape[dim], axis=dim)
        cells = jnp.concatenate(
            [
                lax.ppermute(tail, axis, [(i, (i + 1) % count) for i in range(ends)]),
                cells,
                lax.ppermute(head, axis, [((i + 1) % count, i) for i in range(ends)]),
            ],
            axis=dim,
        )
    return cells


def from_partner(value, axis, distance):
    mask = 2**distance
    pairs = [(source, source ^ mask) for source in range(lax.axis_size(axis))]
    return lax.ppermute(value, axis, pairs)


def operate_padded(padded, padded_k):
    extent_x = padded.shape[1] - 2
    extent_y = padded.shape[2] - 2
    center = padded[:, 1:-1, 1:-1]
    center_k = padded_k[1:-1, 1:-1]
    summed = jnp.zeros_like(center)
    for offset_x, offset_y in ((2, 1), (0, 1), (1, 2), (1, 0)):
        beside = padded[:, offset_x : offset_x + extent_x, offset_y : offset_y + extent_y]
        beside_k = padded_k[offset_x : offset_x + extent_x, offset_y : offset_y + extent_y]
        summed = summed + 0.5 * (center_k + beside_k) * (center - beside)
    return summed


def stencil(values, conductivity):
    stacked = jnp.concatenate([values, conductivity[None]], axis=0)
    padded = extended(stacked, (("gx", 1), ("gy", 2)), 1)
    return operate_padded(padded[:-1], padded[-1])


def leaf_apply(values, leaf_inverse):
    count_s, extent_x, extent_y = values.shape
    blocks_x = extent_x // LBX
    blocks_y = extent_y // LBY
    grouped = values.reshape(count_s, blocks_x, LBX, blocks_y, LBY).transpose(0, 1, 3, 2, 4)
    grouped = grouped.reshape(count_s, blocks_x, blocks_y, LBX * LBY)
    mapped = jnp.einsum("xyij,sxyj->sxyi", leaf_inverse, grouped, precision=HIGHEST)
    mapped = mapped.reshape(count_s, blocks_x, blocks_y, LBX, LBY).transpose(0, 1, 3, 2, 4)
    return mapped.reshape(count_s, extent_x, extent_y)


def spread_tree(coeffs, leaf_transfer, node_transfer, leaf_front, node_front):
    levels = lax.axis_size(("gx", "gy")).bit_length() - 1
    leaf_t = leaf_transfer[0, 0]
    leaf_f = leaf_front[0, 0]
    node_t = node_transfer[0, 0]
    node_f = node_front[0, 0]
    uppers = [coeffs]
    moving = jnp.dot(coeffs, leaf_t, precision=HIGHEST)
    for height in range(1, levels + 1):
        partner = from_partner(moving, ("gx", "gy"), height - 1)
        summed = moving + partner
        uppers.append(summed)
        if height < levels:
            moving = jnp.dot(summed, node_t[height - 1], precision=HIGHEST)
    downward = jnp.dot(uppers[levels], node_f[levels - 1], precision=HIGHEST)
    for height in range(levels, 1, -1):
        downward = jnp.dot(downward, node_t[height - 2].T, precision=HIGHEST) + jnp.dot(
            uppers[height - 1], node_f[height - 2], precision=HIGHEST
        )
    return jnp.dot(downward, leaf_t.T, precision=HIGHEST) + jnp.dot(
        coeffs, leaf_f, precision=HIGHEST
    )


def precondition(
    values, leaf_inverse, front_basis, leaf_transfer, node_transfer, leaf_front, node_front
):
    near = leaf_apply(values, leaf_inverse)
    coeffs = jnp.einsum("sab,abk->sk", values, front_basis, precision=HIGHEST)
    spread = spread_tree(coeffs, leaf_transfer, node_transfer, leaf_front, node_front)
    return near + jnp.einsum("sk,abk->sab", spread, front_basis, precision=HIGHEST)


def on_device(
    right_side,
    conductivity,
    leaf_inverse,
    front_basis,
    leaf_transfer,
    node_transfer,
    leaf_front,
    node_front,
):
    apply_inverse = partial(
        precondition,
        leaf_inverse=leaf_inverse,
        front_basis=front_basis,
        leaf_transfer=leaf_transfer,
        node_transfer=node_transfer,
        leaf_front=leaf_front,
        node_front=node_front,
    )
    first_z = apply_inverse(right_side)
    local_rz = jnp.sum(right_side * first_z, axis=(1, 2))
    rz_old = lax.psum(local_rz, ("gx", "gy"))
    applied = stencil(first_z, conductivity)
    curvature = lax.psum(jnp.sum(first_z * applied, axis=(1, 2)), ("gx", "gy"))
    step_size = (rz_old / curvature)[:, None, None]
    solution = step_size * first_z
    residual = right_side - step_size * applied
    second_z = apply_inverse(residual)
    rz_new = lax.psum(jnp.sum(residual * second_z, axis=(1, 2)), ("gx", "gy"))
    direction = second_z + (rz_new / rz_old)[:, None, None] * first_z
    return (solution, residual, direction)


def solution(mesh):
    return jax.shard_map(
        on_device,
        mesh=mesh,
        in_specs=(
            P(None, "gx", "gy"),
            P("gx", "gy"),
            P("gx", "gy", None, None),
            P("gx", "gy", None),
            P("gx", "gy", None, None),
            P("gx", "gy", None, None, None),
            P("gx", "gy", None, None),
            P("gx", "gy", None, None, None),
        ),
        out_specs=(P(None, "gx", "gy"), P(None, "gx", "gy"), P(None, "gx", "gy")),
        check_vma=False,
    )
```

profile of v0, /device:TPU:1, one launch (start us, length us, event | category | flops | bytes accessed | tf_op | source)
XLA Modules:
  0.0 377.9 jit_solution(12129984315452648051)
XLA Ops:
  3.4 4.4 %collective-permute-start = (f32[2,128]{1,0:T(2,128)S(1)}, f32[2,128]{1,0:T(2,128)S(1)}, u32[]{:S(2)}, u32[]{:S(2)}) collective-permute-start(f32[2,128]{1,0:T(2,128)S(1)} %fusion.94), channel_id=1, source_target_pairs={{0,1},{1,0},{2,3},{3,2},{4,5},{5,4},{6,7},{7,6},{8,9},{9,8},{10,11... | collective-permute-start | bytes 3080 | tf_op jit(solution)/shard_map/ppermute | solution.py:35
  8.8 4.9 %collective-permute-start.1 = (f32[2,128]{1,0:T(2,128)S(1)}, f32[2,128]{1,0:T(2,128)S(1)}, u32[]{:S(2)}, u32[]{:S(2)}) collective-permute-start(f32[2,128]{1,0:T(2,128)S(1)} %fusion.86), channel_id=1, source_target_pairs={{0,2},{1,3},{2,0},{3,1},{4,6},{5,7},{6,4},{7,5},{8,10},{9,11},{10,... | collective-permute-start | bytes 3080 | tf_op jit(solution)/shard_map/ppermute | solution.py:35
  14.9 8.8 %collective-permute-start.2 = (f32[2,128]{1,0:T(2,128)S(1)}, f32[2,128]{1,0:T(2,128)S(1)}, u32[]{:S(2)}, u32[]{:S(2)}) collective-permute-start(f32[2,128]{1,0:T(2,128)S(1)} %fusion.78), channel_id=1, source_target_pairs={{0,4},{1,5},{2,6},{3,7},{4,0},{5,1},{6,2},{7,3},{8,12},{9,13},{10,... | collective-permute-start | bytes 3080 | tf_op jit(solution)/shard_map/ppermute | solution.py:35
  24.8 13.1 %collective-permute-start.3 = (f32[2,128]{1,0:T(2,128)S(1)}, f32[2,128]{1,0:T(2,128)S(1)}, u32[]{:S(2)}, u32[]{:S(2)}) collective-permute-start(f32[2,128]{1,0:T(2,128)S(1)} %fusion.70), channel_id=1, source_target_pairs={{0,8},{1,9},{2,10},{3,11},{4,12},{5,13},{6,14},{7,15},{8,0},{9,1},... | collective-permute-start | bytes 3080 | tf_op jit(solution)/shard_map/ppermute | solution.py:35
  39.0 9.2 %collective-permute-start.4 = (f32[2,128]{1,0:T(2,128)S(1)}, f32[2,128]{1,0:T(2,128)S(1)}, u32[]{:S(2)}, u32[]{:S(2)}) collective-permute-start(f32[2,128]{1,0:T(2,128)S(1)} %fusion.62), channel_id=1, source_target_pairs={{0,16},{1,17},{2,18},{3,19},{4,20},{5,21},{6,22},{7,23},{8,24},{9,... | collective-permute-start | bytes 3080 | tf_op jit(solution)/shard_map/ppermute | solution.py:35
  49.1 1.9 collective-permute-start.5
  51.1 2.4 collective-permute-done.5
  53.6 2.5 collective-permute-start.6
  56.2 3.3 collective-permute-done.6
  59.6 1.9 collective-permute-start.7
  64.1 2.5 collective-permute-start.8
  75.2 6.8 %collective-permute-start.10 = (f32[3,1,128]{2,0,1:T(4,128)S(1)}, f32[3,1,128]{2,0,1:T(4,128)S(1)}, u32[]{:S(2)}, u32[]{:S(2)}) collective-permute-start(f32[3,1,128]{2,0,1:T(4,128)S(1)} %get-tuple-element.18), channel_id=1, source_target_pairs={{16,0},{32,16},{48,32},{64,48},{80,64},{96,80},{112,96},{128,112},... | collective-permute-start | bytes 4616 | tf_op jit(solution)/shard_map/ppermute | solution.py:25
  82.0 1.9 collective-permute-start.9
  88.1 3.4 collective-permute-done.12
  92.7 109.6 %all-reduce = (f32[2]{0:T(128)S(1)}, f32[2]{0:T(128)S(1)}) all-reduce(f32[2]{0:T(128)S(1)} %get-tuple-element.7, f32[2]{0:T(128)S(1)} %get-tuple-element.6), channel_id=1, replica_groups=mesh['gx'=32,'gy'=16] {'gx','gy'}, use_global_device_ids=true, to_apply=%region_1.0 | all-reduce | flops 4 | bytes 32 | tf_op jit(solution)/shard_map/psum | solution.py:122
  204.2 1.9 collective-permute-start.13
  206.2 2.4 collective-permute-done.13
  208.7 1.9 collective-permute-start.14
  210.6 3.3 collective-permute-done.14
  214.1 4.0 %collective-permute-start.15 = (f32[2,128]{1,0:T(2,128)S(1)}, f32[2,128]{1,0:T(2,128)S(1)}, u32[]{:S(2)}, u32[]{:S(2)}) collective-permute-start(f32[2,128]{1,0:T(2,128)S(1)} %fusion.74), channel_id=1, source_target_pairs={{0,4},{1,5},{2,6},{3,7},{4,0},{5,1},{6,2},{7,3},{8,12},{9,13},{10,... | collective-permute-start | bytes 3080 | tf_op jit(solution)/shard_map/ppermute | solution.py:35
  218.1 4.2 %collective-permute-done.15 = f32[2,128]{1,0:T(2,128)S(1)} collective-permute-done((f32[2,128]{1,0:T(2,128)S(1)}, f32[2,128]{1,0:T(2,128)S(1)}, u32[]{:S(2)}, u32[]{:S(2)}) %collective-permute-start.15) | collective-permute-done | bytes 1056 | tf_op jit(solution)/shard_map/ppermute | solution.py:35
  222.5 8.2 %collective-permute-start.16 = (f32[2,128]{1,0:T(2,128)S(1)}, f32[2,128]{1,0:T(2,128)S(1)}, u32[]{:S(2)}, u32[]{:S(2)}) collective-permute-start(f32[2,128]{1,0:T(2,128)S(1)} %fusion.66), channel_id=1, source_target_pairs={{0,8},{1,9},{2,10},{3,11},{4,12},{5,13},{6,14},{7,15},{8,0},{9,1},... | collective-permute-start | bytes 3080 | tf_op jit(solution)/shard_map/ppermute | solution.py:35
  230.7 4.8 %collective-permute-done.16 = f32[2,128]{1,0:T(2,128)S(1)} collective-permute-done((f32[2,128]{1,0:T(2,128)S(1)}, f32[2,128]{1,0:T(2,128)S(1)}, u32[]{:S(2)}, u32[]{:S(2)}) %collective-permute-start.16) | collective-permute-done | bytes 1056 | tf_op jit(solution)/shard_map/ppermute | solution.py:35
  236.0 7.7 %collective-permute-start.17 = (f32[2,128]{1,0:T(2,128)S(1)}, f32[2,128]{1,0:T(2,128)S(1)}, u32[]{:S(2)}, u32[]{:S(2)}) collective-permute-start(f32[2,128]{1,0:T(2,128)S(1)} %fusion.58), channel_id=1, source_target_pairs={{0,16},{1,17},{2,18},{3,19},{4,20},{5,21},{6,22},{7,23},{8,24},{9,... | collective-permute-start | bytes 3080 | tf_op jit(solution)/shard_map/ppermute | solution.py:35
  245.1 1.9 collective-permute-start.18
  247.0 2.4 collective-permute-done.18
  250.0 2.5 collective-permute-start.19
  252.5 3.3 collective-permute-done.19
  256.3 1.9 collective-permute-start.20
  258.5 2.2 collective-permute-done.20
  261.6 2.8 collective-permute-start.21
  274.6 101.4 %psum.23 = f32[2]{0:T(128)S(1)} all-reduce(f32[2]{0:T(128)S(1)} %get-tuple-element.21), channel_id=1, replica_groups=mesh['gx'=32,'gy'=16] {'gx','gy'}, use_global_device_ids=true, to_apply=%region_5.0 | all-reduce | flops 2 | bytes 16 | tf_op jit(solution)/shard_map/psum | solution.py:129
  (142 shorter events, 43.3 us)
Async XLA Ops:
  0.6 1.2 copy-start
  0.6 2.5 copy-start.4
  0.7 8.0 %copy-start.1 = (f32[1,1,8,128,128]{4,3,2,1,0:T(8,128)S(1)}, f32[1,1,8,128,128]{4,3,2,1,0:T(8,128)}, u32[]{:S(2)}) copy-start(f32[1,1,8,128,128]{4,3,2,1,0:T(8,128)} %param.13) | copy-start | bytes 1572868
  0.7 65.9 %copy-start.2 = (f32[4,4,128,128]{3,2,1,0:T(8,128)S(1)}, f32[4,4,128,128]{3,2,1,0:T(8,128)}, u32[]{:S(2)}) copy-start(f32[4,4,128,128]{3,2,1,0:T(8,128)} %param.10) | copy-start | bytes 3145732
  3.4 5.3 %collective-permute-start = (f32[2,128]{1,0:T(2,128)S(1)}, f32[2,128]{1,0:T(2,128)S(1)}, u32[]{:S(2)}, u32[]{:S(2)}) collective-permute-start(f32[2,128]{1,0:T(2,128)S(1)} %fusion.94), channel_id=1, source_target_pairs={{0,1},{1,0},{2,3},{3,2},{4,5},{5,4},{6,7},{7,6},{8,9},{9,8},{10,11... | collective-permute-start | bytes 3080 | tf_op jit(solution)/shard_map/ppermute | solution.py:35
  8.8 5.9 %collective-permute-start.1 = (f32[2,128]{1,0:T(2,128)S(1)}, f32[2,128]{1,0:T(2,128)S(1)}, u32[]{:S(2)}, u32[]{:S(2)}) collective-permute-start(f32[2,128]{1,0:T(2,128)S(1)} %fusion.86), channel_id=1, source_target_pairs={{0,2},{1,3},{2,0},{3,1},{4,6},{5,7},{6,4},{7,5},{8,10},{9,11},{10,... | collective-permute-start | bytes 3080 | tf_op jit(solution)/shard_map/ppermute | solution.py:35
  14.9 9.8 %collective-permute-start.2 = (f32[2,128]{1,0:T(2,128)S(1)}, f32[2,128]{1,0:T(2,128)S(1)}, u32[]{:S(2)}, u32[]{:S(2)}) collective-permute-start(f32[2,128]{1,0:T(2,128)S(1)} %fusion.78), channel_id=1, source_target_pairs={{0,4},{1,5},{2,6},{3,7},{4,0},{5,1},{6,2},{7,3},{8,12},{9,13},{10,... | collective-permute-start | bytes 3080 | tf_op jit(solution)/shard_map/ppermute | solution.py:35
  24.8 14.0 %collective-permute-start.3 = (f32[2,128]{1,0:T(2,128)S(1)}, f32[2,128]{1,0:T(2,128)S(1)}, u32[]{:S(2)}, u32[]{:S(2)}) collective-permute-start(f32[2,128]{1,0:T(2,128)S(1)} %fusion.70), channel_id=1, source_target_pairs={{0,8},{1,9},{2,10},{3,11},{4,12},{5,13},{6,14},{7,15},{8,0},{9,1},... | collective-permute-start | bytes 3080 | tf_op jit(solution)/shard_map/ppermute | solution.py:35
  39.0 10.0 %collective-permute-start.4 = (f32[2,128]{1,0:T(2,128)S(1)}, f32[2,128]{1,0:T(2,128)S(1)}, u32[]{:S(2)}, u32[]{:S(2)}) collective-permute-start(f32[2,128]{1,0:T(2,128)S(1)} %fusion.62), channel_id=1, source_target_pairs={{0,16},{1,17},{2,18},{3,19},{4,20},{5,21},{6,22},{7,23},{8,24},{9,... | collective-permute-start | bytes 3080 | tf_op jit(solution)/shard_map/ppermute | solution.py:35
  49.1 4.3 %collective-permute-start.5 = (f32[2,128]{1,0:T(2,128)S(1)}, f32[2,128]{1,0:T(2,128)S(1)}, u32[]{:S(2)}, u32[]{:S(2)}) collective-permute-start(f32[2,128]{1,0:T(2,128)S(1)} %fusion.54), channel_id=1, source_target_pairs={{0,32},{1,33},{2,34},{3,35},{4,36},{5,37},{6,38},{7,39},{8,40},{9,... | collective-permute-start | bytes 3080 | tf_op jit(solution)/shard_map/ppermute | solution.py:35
  53.6 5.8 %collective-permute-start.6 = (f32[2,128]{1,0:T(2,128)S(1)}, f32[2,128]{1,0:T(2,128)S(1)}, u32[]{:S(2)}, u32[]{:S(2)}) collective-permute-start(f32[2,128]{1,0:T(2,128)S(1)} %fusion.46), channel_id=1, source_target_pairs={{0,64},{1,65},{2,66},{3,67},{4,68},{5,69},{6,70},{7,71},{8,72},{9,... | collective-permute-start | bytes 3080 | tf_op jit(solution)/shard_map/ppermute | solution.py:35
  59.6 4.3 %collective-permute-start.7 = (f32[2,128]{1,0:T(2,128)S(1)}, f32[2,128]{1,0:T(2,128)S(1)}, u32[]{:S(2)}, u32[]{:S(2)}) collective-permute-start(f32[2,128]{1,0:T(2,128)S(1)} %fusion.38), channel_id=1, source_target_pairs={{0,128},{1,129},{2,130},{3,131},{4,132},{5,133},{6,134},{7,135},{8... | collective-permute-start | bytes 3080 | tf_op jit(solution)/shard_map/ppermute | solution.py:35
  64.1 6.0 %copy-start.3 = (f32[1,1,9,128,128]{4,3,2,1,0:T(8,128)S(1)}, f32[1,1,9,128,128]{4,3,2,1,0:T(8,128)}, u32[]{:S(2)}) copy-start(f32[1,1,9,128,128]{4,3,2,1,0:T(8,128)} %param.15) | copy-start | bytes 1769476
  64.1 6.0 %collective-permute-start.8 = (f32[2,128]{1,0:T(2,128)S(1)}, f32[2,128]{1,0:T(2,128)S(1)}, u32[]{:S(2)}, u32[]{:S(2)}) collective-permute-start(f32[2,128]{1,0:T(2,128)S(1)} %fusion.30), channel_id=1, source_target_pairs={{0,256},{1,257},{2,258},{3,259},{4,260},{5,261},{6,262},{7,263},{8... | collective-permute-start | bytes 3080 | tf_op jit(solution)/shard_map/ppermute | solution.py:35
  73.1 0.9 copy-start.6
  74.2 1.0 copy-start.7
  75.2 8.8 %collective-permute-start.10 = (f32[3,1,128]{2,0,1:T(4,128)S(1)}, f32[3,1,128]{2,0,1:T(4,128)S(1)}, u32[]{:S(2)}, u32[]{:S(2)}) collective-permute-start(f32[3,1,128]{2,0,1:T(4,128)S(1)} %get-tuple-element.18), channel_id=1, source_target_pairs={{16,0},{32,16},{48,32},{64,48},{80,64},{96,80},{112,96},{128,112},... | collective-permute-start | bytes 4616 | tf_op jit(solution)/shard_map/ppermute | solution.py:25
  82.0 3.1 collective-permute-start.9
  85.2 3.0 collective-permute-start.11
  86.8 4.7 %collective-permute-start.12 = (f32[3,18,1]{2,0,1:T(4,128)S(1)}, f32[3,18,1]{2,0,1:T(4,128)S(1)}, u32[]{:S(2)}, u32[]{:S(2)}) collective-permute-start(f32[3,18,1]{2,0,1:T(4,128)S(1)} %get-tuple-element.11), channel_id=1, source_target_pairs={{1,0},{2,1},{3,2},{4,3},{5,4},{6,5},{7,6},{8,7},{9,8},{10,9},{11,1... | collective-permute-start | bytes 656 | tf_op jit(solution)/shard_map/ppermute | solution.py:25
  91.7 0.7 copy-start.5
  204.2 4.3 %collective-permute-start.13 = (f32[2,128]{1,0:T(2,128)S(1)}, f32[2,128]{1,0:T(2,128)S(1)}, u32[]{:S(2)}, u32[]{:S(2)}) collective-permute-start(f32[2,128]{1,0:T(2,128)S(1)} %fusion.90), channel_id=1, source_target_pairs={{0,1},{1,0},{2,3},{3,2},{4,5},{5,4},{6,7},{7,6},{8,9},{9,8},{10,11... | collective-permute-start | bytes 3080 | tf_op jit(solution)/shard_map/ppermute | solution.py:35
  208.7 5.2 %collective-permute-start.14 = (f32[2,128]{1,0:T(2,128)S(1)}, f32[2,128]{1,0:T(2,128)S(1)}, u32[]{:S(2)}, u32[]{:S(2)}) collective-permute-start(f32[2,128]{1,0:T(2,128)S(1)} %fusion.82), channel_id=1, source_target_pairs={{0,2},{1,3},{2,0},{3,1},{4,6},{5,7},{6,4},{7,5},{8,10},{9,11},{10,... | collective-permute-start | bytes 3080 | tf_op jit(solution)/shard_map/ppermute | solution.py:35
  214.1 8.2 %collective-permute-start.15 = (f32[2,128]{1,0:T(2,128)S(1)}, f32[2,128]{1,0:T(2,128)S(1)}, u32[]{:S(2)}, u32[]{:S(2)}) collective-permute-start(f32[2,128]{1,0:T(2,128)S(1)} %fusion.74), channel_id=1, source_target_pairs={{0,4},{1,5},{2,6},{3,7},{4,0},{5,1},{6,2},{7,3},{8,12},{9,13},{10,... | collective-permute-start | bytes 3080 | tf_op jit(solution)/shard_map/ppermute | solution.py:35
  222.5 13.0 %collective-permute-start.16 = (f32[2,128]{1,0:T(2,128)S(1)}, f32[2,128]{1,0:T(2,128)S(1)}, u32[]{:S(2)}, u32[]{:S(2)}) collective-permute-start(f32[2,128]{1,0:T(2,128)S(1)} %fusion.66), channel_id=1, source_target_pairs={{0,8},{1,9},{2,10},{3,11},{4,12},{5,13},{6,14},{7,15},{8,0},{9,1},... | collective-permute-start | bytes 3080 | tf_op jit(solution)/shard_map/ppermute | solution.py:35
  236.0 8.5 %collective-permute-start.17 = (f32[2,128]{1,0:T(2,128)S(1)}, f32[2,128]{1,0:T(2,128)S(1)}, u32[]{:S(2)}, u32[]{:S(2)}) collective-permute-start(f32[2,128]{1,0:T(2,128)S(1)} %fusion.58), channel_id=1, source_target_pairs={{0,16},{1,17},{2,18},{3,19},{4,20},{5,21},{6,22},{7,23},{8,24},{9,... | collective-permute-start | bytes 3080 | tf_op jit(solution)/shard_map/ppermute | solution.py:35
  245.1 4.3 %collective-permute-start.18 = (f32[2,128]{1,0:T(2,128)S(1)}, f32[2,128]{1,0:T(2,128)S(1)}, u32[]{:S(2)}, u32[]{:S(2)}) collective-permute-start(f32[2,128]{1,0:T(2,128)S(1)} %fusion.50), channel_id=1, source_target_pairs={{0,32},{1,33},{2,34},{3,35},{4,36},{5,37},{6,38},{7,39},{8,40},{9,... | collective-permute-start | bytes 3080 | tf_op jit(solution)/shard_map/ppermute | solution.py:35
  250.0 5.8 %collective-permute-start.19 = (f32[2,128]{1,0:T(2,128)S(1)}, f32[2,128]{1,0:T(2,128)S(1)}, u32[]{:S(2)}, u32[]{:S(2)}) collective-permute-start(f32[2,128]{1,0:T(2,128)S(1)} %fusion.42), channel_id=1, source_target_pairs={{0,64},{1,65},{2,66},{3,67},{4,68},{5,69},{6,70},{7,71},{8,72},{9,... | collective-permute-start | bytes 3080 | tf_op jit(solution)/shard_map/ppermute | solution.py:35
  256.3 4.4 %collective-permute-start.20 = (f32[2,128]{1,0:T(2,128)S(1)}, f32[2,128]{1,0:T(2,128)}, u32[]{:S(2)}, u32[]{:S(2)}) collective-permute-start(f32[2,128]{1,0:T(2,128)S(1)} %fusion.34), channel_id=1, source_target_pairs={{0,128},{1,129},{2,130},{3,131},{4,132},{5,133},{6,134},{7,135},{8... | collective-permute-start | bytes 3080 | tf_op jit(solution)/shard_map/ppermute | solution.py:35
  261.6 5.8 %collective-permute-start.21 = (f32[2,128]{1,0:T(2,128)S(1)}, f32[2,128]{1,0:T(2,128)S(1)}, u32[]{:S(2)}, u32[]{:S(2)}) collective-permute-start(f32[2,128]{1,0:T(2,128)S(1)} %fusion.26), channel_id=1, source_target_pairs={{0,256},{1,257},{2,258},{3,259},{4,260},{5,261},{6,262},{7,263},{8... | collective-permute-start | bytes 3080 | tf_op jit(solution)/shard_map/ppermute | solution.py:35
  268.6 0.7 copy-start.15
  274.6 101.4 %copy-start.19 = (f32[2]{0:T(128)S(1)}, f32[2]{0:T(128)}, u32[]{:S(2)}) copy-start(f32[2]{0:T(128)} %copy-done.18) | copy-start | bytes 28
  (10 other events, 6.0 us)
where the time goes:
time: 379 us; the launch traced here: 378 us
  blocking collectives  211 us (56%)
  starting transfers between devices  93.8 us (25%)
  waiting for transfers between devices  41.5 us (11%)
  matrix products  18.7 us (5%)
  local copies, waits for them, and re-layouts  11.2 us (3%)
    psum x1, blocking collectives, on_device(): rz_old = lax.psum(local_rz, ('gx', 'gy'))  110 us
    psum x1, blocking collectives, on_device(): rz_new = lax.psum(jnp.sum(residual * second_z, axis=(1, 2)), ('gx', 'gy'))  101 us
    ppermute x18, starting transfers between devices, from_partner(): return lax.ppermute(value, axis, pairs)  82.1 us
    ppermute x18, waiting for transfers between devices, from_partner(): return lax.ppermute(value, axis, pairs)  37 us
    unnamed x44, local copies, waits for them, and re-layouts  9.48 us
    ppermute x2, starting transfers between devices, extended(): lax.ppermute(head, axis, [((i + 1) % count, i) for i in range(ends)])  8.12 us
  transfers between devices with their start and end apart: 22, of which 20 were waited for; matrix products, arithmetic and copies ran while one was open for 2% of the time, Pallas kernels for 0%

commit v1 on v0

v1 whole, which is shorter than its diff:
```python
import jax
import jax.numpy as jnp
from jax import lax
from jax.experimental import pallas as pl
from jax.experimental.pallas import tpu as pltpu
from jax.sharding import PartitionSpec as P

HIGHEST = lax.Precision.HIGHEST
MESH = pl.DeviceIdType.MESH
F32 = jnp.float32
K = 128


def dot(a, b):
    return lax.dot_general(
        a, b, (((1,), (0,)), ((), ())), precision=HIGHEST, preferred_element_type=F32
    )


def dot_t(a, b):
    return lax.dot_general(
        a, b, (((1,), (1,)), ((), ())), precision=HIGHEST, preferred_element_type=F32
    )


def units(extra):
    return {d: 5 - d.bit_length() + extra for d in range(1, 16)}


def offsets(count):
    at, out = 0, {}
    for d in sorted(count):
        out[d] = at
        at += count[d]
    return out, at


def butterfly(values):
    while len(values) > 1:
        values = [values[i] + values[i + 1] for i in range(0, len(values), 2)]
    return values[0]


ORDER = (8, 15, 14, 13, 12, 11, 10, 9, 7, 6, 5, 4, 3, 2, 1)


def tile_rows(x):
    return jnp.concatenate([x, x], axis=0)


def shuffle(t):
    row = lax.broadcasted_iota(jnp.int32, t.shape, 0) % 4
    chunk = lax.broadcasted_iota(jnp.int32, t.shape, 1) // 32
    rows, lanes = t.shape
    out = t
    for delta in (-3, -2, -1, 1, 2, 3):
        moved = pltpu.roll(t, delta % rows, 0)
        moved = pltpu.roll(moved, (-32 * delta) % lanes, 1)
        out = jnp.where(row - chunk == delta, moved, out)
    return out


def kernel(
    rs_h, cond_h, linv_h, basis_h, e0_h, nt_h, f0_h, nf_h,
    sol_o, res_o, dir_o,
    rs, cond, linv, basis, e0, nt, f0, nf,
    pu, ru, gs, lb, wt, tmp,
    zs1, zb1, zs2, zb2, zs3, zb3,
    cs1, cb1, cs2, cb2, cs3, cb3,
    gs1, gb1, gs2, gb2, gs3, gb3,
    hrs, hrb, hcs, hcb, krs, krb, kcs, kcb,
    lsem, ssem, rsem, hsem, hrsem,
):
    X = lax.axis_index("gx")
    Z = lax.axis_index("gy")
    z_peer = lambda d: (X, Z ^ d)
    c_peer = (X ^ 1, Z)
    g_peer = lambda d: (X ^ (2 * d), Z)
    x_up, x_down = (X + 1) % 32, (X + 31) % 32
    z_up, z_down = (Z + 1) % 16, (Z + 15) % 16

    barrier = pltpu.get_barrier_semaphore()
    others = [z_peer(d) for d in ORDER] + [g_peer(d) for d in ORDER] + [c_peer]
    halo = [(x_up, Z), (x_down, Z), (X, z_up), (X, z_down)]
    for who in others + halo:
        pl.semaphore_signal(barrier, inc=1, device_id=who, device_id_type=MESH)

    loads = {}
    for i, (name, src, dst) in enumerate(
        (
            ("e0", e0_h.at[0, 0], e0),
            ("nt", nt_h.at[0, 0], nt),
            ("rs", rs_h, rs),
            ("basis", basis_h, basis),
            ("cond", cond_h, cond),
            ("f0", f0_h.at[0, 0], f0),
            ("nf", nf_h.at[0, 0], nf),
            ("linv", linv_h, linv),
        )
    ):
        loads[name] = pltpu.make_async_copy(src, dst, lsem.at[i])
        loads[name].start()

    def send(src, dst, sends, recvs, who):
        copy = pltpu.make_async_remote_copy(
            src_ref=src, dst_ref=dst, send_sem=sends, recv_sem=recvs,
            device_id=who, device_id_type=MESH,
        )
        copy.start()
        return copy

    def send_group(src, buf, extra, slot, peer):
        count = units(extra)
        at, _ = offsets(count)
        for d in ORDER:
            n = count[d]
            send(
                src.at[pl.ds(0, n)], buf.at[pl.ds(at[d], n)], ssem.at[slot], rsem.at[slot], peer(d)
            )

    def wait_bytes(buf, sem):
        pltpu.make_async_copy(buf, buf, sem).wait()

    def group_sums(src, buf, extra):
        count = units(extra)
        at, _ = offsets(count)
        out = []
        for unit in range(4 + extra):
            reach = [d for d in range(1, 16) if count[d] > unit]
            out.append(butterfly([src[unit]] + [buf[at[d] + unit] for d in reach]))
        return out

    row = lax.broadcasted_iota(jnp.int32, (32, K), 0)
    lane = lax.broadcasted_iota(jnp.int32, (32, K), 1)

    def send_edges(t, rows_src, rows_buf, cols_src, cols_buf, first):
        rows_src[0] = jnp.concatenate([t[15:16], t[31:32]], axis=0)
        rows_src[1] = jnp.concatenate([t[0:1], t[16:17]], axis=0)
        lane8 = lane[0:8]
        last_col = pltpu.roll(t[0:8], 1, 1)
        first_col = t[0:8]
        for j in range(1, 4):
            part = t[8 * j : 8 * j + 8]
            last_col = jnp.where(lane8 == j, pltpu.roll(part, j + 1, 1), last_col)
            first_col = jnp.where(lane8 == j, pltpu.roll(part, j, 1), first_col)
        cols_src[0] = last_col
        cols_src[1] = first_col
        return [
            send(rows_src.at[0], rows_buf.at[0], hsem.at[first], hrsem.at[first], (x_up, Z)),
            send(rows_src.at[1], rows_buf.at[1], hsem.at[first + 1], hrsem.at[first + 1], (x_down, Z)),
            send(cols_src.at[0], cols_buf.at[0], hsem.at[first + 2], hrsem.at[first + 2], (X, z_up)),
            send(cols_src.at[1], cols_buf.at[1], hsem.at[first + 3], hrsem.at[first + 3], (X, z_down)),
        ]

    def beside(t, rows_buf, cols_buf):
        def spread(h):
            return jnp.concatenate(
                [jnp.broadcast_to(h[0:1], (16, K)), jnp.broadcast_to(h[1:2], (16, K))], axis=0
            )

        low = spread(jnp.where(X > 0, rows_buf[0], 0.0))
        high = spread(jnp.where(X < 31, rows_buf[1], 0.0))
        left = jnp.where(Z > 0, cols_buf[0], 0.0)
        right = jnp.where(Z < 15, cols_buf[1], 0.0)
        left = jnp.concatenate([left] + [pltpu.roll(left, K - j, 1) for j in range(1, 4)], axis=0)
        right = jnp.concatenate([pltpu.roll(right, K - 1 - j, 1) for j in range(4)], axis=0)
        return (
            jnp.where(row % 16 == 15, high, pltpu.roll(t, 31, 0)),
            jnp.where(row % 16 == 0, low, pltpu.roll(t, 1, 0)),
            jnp.where(lane == K - 1, right, pltpu.roll(t, K - 1, 1)),
            jnp.where(lane == 0, left, pltpu.roll(t, 1, 1)),
        )

    def flat_rows(ref):
        return jnp.concatenate([ref[:, x, :] for x in range(16)], axis=1)

    def coefficients(ref):
        return dot(flat_rows(ref), basis[...].reshape(16 * K, K))

    def leaf_apply(t):
        g = shuffle(t)
        for i in range(16):
            lhs = jnp.concatenate([g[i : i + 1], g[16 + i : 17 + i]], axis=0)
            out = dot(lhs, linv[i // 4, i % 4])
            tmp[pl.ds(i, 1)] = out[0:1]
            tmp[pl.ds(16 + i, 1)] = out[1:2]
        return shuffle(tmp[...])

    def spread_out(y):
        w = dot_t(y, basis[...].reshape(16 * K, K))
        for x in range(16):
            wt[:, x, :] = w[:, x * K : (x + 1) * K]
        return wt[...].reshape(32, K)

    def put(ref, rows2, first=0):
        for i in range(rows2.shape[1] // K):
            ref[first + i] = rows2[:, i * K : (i + 1) * K]

    loads["e0"].wait()
    loads["nt"].wait()
    p = e0[...]
    pu[:, 3 * K : 4 * K] = p
    for i in range(3):
        p = dot(p, nt[i])
        pu[:, (2 - i) * K : (3 - i) * K] = p
    loads["rs"].wait()
    loads["basis"].wait()
    u0 = coefficients(rs)
    put(zs1, dot(u0, pu[...]))
    pl.semaphore_wait(barrier, len(others) + len(halo))
    send_group(zs1, zb1, 0, 0, z_peer)

    loads["cond"].wait()
    k32 = tile_rows(cond[...])
    edges_k = send_edges(k32, krs, krb, kcs, kcb, 0)
    r = nt[3]
    ru[:, 4 * K : 5 * K] = r
    for i in range(4):
        r = dot(r, nt[4 + i])
        ru[:, (3 - i) * K : (4 - i) * K] = r
    loads["f0"].wait()
    loads["nf"].wait()
    gs[0:K] = f0[...]
    for h in range(1, 5):
        gs[h * K : (h + 1) * K] = dot_t(nf[h - 1], pu[:, (4 - h) * K : (5 - h) * K])
    loads["linv"].wait()
    b32 = rs[...].reshape(32, K)
    lb[...] = leaf_apply(b32)

    def up_z(buf, src, extra, slot):
        wait_bytes(buf, rsem.at[slot])
        return group_sums(src, buf, extra)

    def core_round(src, buf, slot):
        copy = send(src, buf, ssem.at[slot], rsem.at[slot], c_peer)
        copy.wait_recv()
        return copy, src[...] + buf[...]

    u4, u3, u2, u1 = up_z(zb1, zs1, 0, 0)
    put(cs1, dot(u4, ru[...]))
    core1, c = core_round(cs1, cb1, 1)
    u5 = c[4]
    gs1[...] = c[0:4]
    send_group(gs1, gb1, 0, 2, g_peer)
    for h in range(5, 10):
        g = dot_t(nf[h - 1], ru[:, (9 - h) * K : (10 - h) * K])
        gs[h * K : (h + 1) * K] = dot_t(g, pu[:, 0:K])
    y = dot(jnp.concatenate([u0, u1, u2, u3, u4, u5], axis=1), gs[0 : 6 * K])
    for e in edges_k:
        e.wait_recv()
    weights = [0.5 * (k32 + other) for other in beside(k32, krb, kcb)]
    u9, u8, u7, u6 = up_z(gb1, gs1, 0, 2)
    y = y + dot(jnp.concatenate([u6, u7, u8, u9], axis=1), gs[6 * K : 10 * K])
    z = lb[...] + spread_out(y)

    edges_z = send_edges(z, hrs, hrb, hcs, hcb, 4)
    for e in edges_z:
        e.wait_recv()
    applied = jnp.zeros_like(z)
    for weight, other in zip(weights, beside(z, hrb, hcb)):
        applied = applied + weight * (z - other)
    res_o[...] = applied.reshape(2, 16, K)

    def total(t):
        return jnp.sum(t.reshape(2, 16, K), axis=(1, 2), keepdims=True)[:, 0]

    lane2 = lane[0:2]
    u0 = coefficients(res_o)
    zs2[0] = jnp.where(
        lane2 == 0, total(b32 * z), jnp.where(lane2 == 1, total(z * applied), 0.0)
    )
    put(zs2, dot(u0, pu[...]), 1)
    send_group(zs2, zb2, 1, 3, z_peer)
    near = leaf_apply(applied)
    s0, u4, u3, u2, u1 = up_z(zb2, zs2, 1, 3)
    cs2[0] = s0
    put(cs2, dot(u4, ru[...]), 1)
    core2, c = core_round(cs2, cb2, 4)
    u5 = c[5]
    gs2[...] = c[0:5]
    send_group(gs2, gb2, 1, 5, g_peer)
    y = dot(jnp.concatenate([u0, u1, u2, u3, u4, u5], axis=1), gs[0 : 6 * K])
    s0, u9, u8, u7, u6 = up_z(gb2, gs2, 1, 5)
    y = y + dot(jnp.concatenate([u6, u7, u8, u9], axis=1), gs[6 * K : 10 * K])
    mapped = near + spread_out(y)

    rz_old = s0[:, 0:1]
    step = rz_old / s0[:, 1:2]
    step32 = jnp.concatenate(
        [jnp.broadcast_to(step[0:1], (16, K)), jnp.broadcast_to(step[1:2], (16, K))], axis=0
    )
    residual = b32 - step32 * applied
    second = z - step32 * mapped
    zs3[0] = jnp.broadcast_to(total(residual * second), (2, K))
    for d in ORDER:
        send(zs3, zb3.at[pl.ds(d - 1, 1)], ssem.at[6], rsem.at[6], z_peer(d))
    sol_o[...] = (step32 * z).reshape(2, 16, K)
    res_o[...] = residual.reshape(2, 16, K)
    wait_bytes(zb3, rsem.at[6])
    cs3[0] = butterfly([zs3[0]] + [zb3[d] for d in range(15)])
    core3, c = core_round(cs3, cb3, 7)
    gs3[...] = c
    for d in ORDER:
        send(gs3, gb3.at[pl.ds(d - 1, 1)], ssem.at[8], rsem.at[8], g_peer(d))
    wait_bytes(gb3, rsem.at[8])
    rz_new = butterfly([gs3[0]] + [gb3[d] for d in range(15)])
    ratio = rz_new / rz_old
    ratio32 = jnp.concatenate(
        [jnp.broadcast_to(ratio[0:1], (16, K)), jnp.broadcast_to(ratio[1:2], (16, K))], axis=0
    )
    dir_o[...] = (second + ratio32 * z).reshape(2, 16, K)

    for e in edges_k + edges_z + [core1, core2, core3]:
        e.wait_send()
    for buf, slot in ((zb1, 0), (gb1, 2), (zb2, 3), (gb2, 5), (zb3, 6), (gb3, 8)):
        wait_bytes(buf, ssem.at[slot])


def on_device(*args):
    unit = lambda n: pltpu.VMEM((n, 2, K), F32)
    square = lambda *n: pltpu.VMEM(n + (K, K), F32)
    out = jax.ShapeDtypeStruct((2, 16, K), F32)
    return pl.pallas_call(
        kernel,
        name="pcg_step",
        out_shape=(out, out, out),
        in_specs=[pl.BlockSpec(memory_space=pl.ANY)] * 8,
        out_specs=[pl.BlockSpec(memory_space=pltpu.VMEM)] * 3,
        scratch_shapes=[
            pltpu.VMEM((2, 16, K), F32), pltpu.VMEM((16, K), F32), square(4, 4), square(16),
            square(), square(8), square(), square(9),
            pltpu.VMEM((K, 4 * K), F32), pltpu.VMEM((K, 5 * K), F32), pltpu.VMEM((10 * K, K), F32),
            pltpu.VMEM((32, K), F32), pltpu.VMEM((2, 16, K), F32), pltpu.VMEM((32, K), F32),
            unit(4), unit(26), unit(5), unit(41), unit(1), unit(15),
            unit(5), unit(5), unit(6), unit(6), unit(1), unit(1),
            unit(4), unit(26), unit(5), unit(41), unit(1), unit(15),
            unit(2), unit(2), pltpu.VMEM((2, 8, K), F32), pltpu.VMEM((2, 8, K), F32),
            unit(2), unit(2), pltpu.VMEM((2, 8, K), F32), pltpu.VMEM((2, 8, K), F32),
            pltpu.SemaphoreType.DMA((8,)), pltpu.SemaphoreType.DMA((9,)),
            pltpu.SemaphoreType.DMA((9,)), pltpu.SemaphoreType.DMA((8,)),
            pltpu.SemaphoreType.DMA((8,)),
        ],
        compiler_params=pltpu.CompilerParams(
            collective_id=0, has_side_effects=True, vmem_limit_bytes=60 * 1024 * 1024
        ),
    )(*args)


def solution(mesh):
    return jax.shard_map(
        on_device,
        mesh=mesh,
        in_specs=(
            P(None, "gx", "gy"),
            P("gx", "gy"),
            P("gx", "gy", None, None),
            P("gx", "gy", None),
            P("gx", "gy", None, None),
            P("gx", "gy", None, None, None),
            P("gx", "gy", None, None),
            P("gx", "gy", None, None, None),
        ),
        out_specs=(P(None, "gx", "gy"), P(None, "gx", "gy"), P(None, "gx", "gy")),
        check_vma=False,
    )
```

time: 379 us -> 64.5 us (0.17)
  blocking collectives: 211 us -> 0 us
  starting transfers between devices: 93.8 us -> 0 us
  Pallas kernels: 0 us -> 60.9 us
  waiting for transfers between devices: 41.5 us -> 0 us
  matrix products: 18.7 us -> 0 us
  local copies, waits for them, and re-layouts: 11.2 us -> 2.66 us
    psum x2 -> x0, blocking collectives: 211 us -> none  [the longest x1 110 us: on_device(): rz_old = lax.psum(local_rz, ('gx', 'gy'))]
    ppermute x22 -> x0, starting transfers between devices: 93.8 us -> none  [the longest x18 82.1 us: from_partner(): return lax.ppermute(value, axis, pairs)]
    pallas_call x0 -> x1, Pallas kernels: none -> 60.9 us  [on_device(): pl.pallas_call(kernel, name='pcg_step', out_shape=(out, out, out), in_spe...]
    ppermute x22 -> x0, waiting for transfers between devices: 41.5 us -> none  [the longest x18 37 us: from_partner(): return lax.ppermute(value, axis, pairs)]
    dot_general x62 -> x0, matrix products: 18.7 us -> none  [the longest x16 3.67 us: spread_tree(): jnp.dot(uppers[height - 1], node_f[height - 2], precision=HIGHEST)]
    unnamed x44 -> x7, local copies, waits for them, and re-layouts: 9.48 us -> 2.66 us
  transfers between devices with their start and end apart: 22 -> 0, of which waited for: 20 -> 0; matrix products, arithmetic and copies ran while one was open for 2% -> 0% of each run, Pallas kernels for 0% -> 0%
where the time goes in v1:
time: 64.5 us; the launch traced here: 64.2 us
  Pallas kernels  60.9 us (94%)
  local copies, waits for them, and re-layouts  2.66 us (4%)
  between operations  0.65 us (1%)
    pallas_call x1, Pallas kernels, on_device(): pl.pallas_call(kernel, name='pcg_step', out_shape=(out, out, out), in_spe...  60.9 us
    unnamed x7, local copies, waits for them, and re-layouts  2.66 us

profile of v1, /device:TPU:1, one launch (start us, length us, event | category | flops | bytes accessed | tf_op | source)
XLA Modules:
  0.0 64.2 jit_solution(6122339363136362552)
XLA Ops:
  0.6 60.9 %pcg_step.1 = (f32[2,16,128]{2,1,0:T(8,128)}, f32[2,16,128]{2,1,0:T(8,128)}, f32[2,16,128]{2,1,0:T(8,128)}) custom-call(f32[2,16,128]{2,1,0:T(8,128)} %rs_h.1, f32[16,128]{1,0:T(8,128)} %cond_h.1, f32[4,4,128,128]{3,2,1,0:T(8,128)} %linv_h.1, f32[16,128,128]{2,1,0:T(8,128)} %basis_h.1, f32[1,1,128,128]{3,2,1,0:T(8,128)} %e0_h.1, ...), custom_call_target="tpu_custom_call" | custom-call | tf_op jit(solution)/shard_map/pcg_step/pallas_call | solution.py:323
  61.5 0.0 copy-start.1
  61.6 1.3 %copy.14 = f32[2,16,128]{2,1,0:T(8,128)} copy(f32[2,16,128]{2,1,0:T(8,128)} %get-tuple-element.6) | data formatting | bytes 32768
  62.9 0.0 copy-done.1
  62.9 0.0 copy-start
  62.9 0.6 copy.15
  63.5 0.1 copy-done
  63.6 0.6 copy.16
Async XLA Ops:
  61.5 1.3 %copy-start.1 = (f32[2,16,128]{2,1,0:T(8,128)S(1)}, f32[2,16,128]{2,1,0:T(8,128)}, u32[]{:S(2)}) copy-start(f32[2,16,128]{2,1,0:T(8,128)} %get-tuple-element.7) | copy-start | bytes 49156
  62.9 0.7 %copy-start = (f32[2,16,128]{2,1,0:T(8,128)S(1)}, f32[2,16,128]{2,1,0:T(8,128)}, u32[]{:S(2)}) copy-start(f32[2,16,128]{2,1,0:T(8,128)} %get-tuple-element.8) | copy-start | bytes 49156

commit v2 on v1

v2 whole, which is shorter than its diff:
```python
import jax
import jax.numpy as jnp
from jax import lax
from jax.experimental import pallas as pl
from jax.experimental.pallas import tpu as pltpu
from jax.sharding import PartitionSpec as P

HIGHEST = lax.Precision.HIGHEST
MESH = pl.DeviceIdType.MESH
F32 = jnp.float32
BF16 = jnp.bfloat16
K = 128


def dot(a, b):
    return lax.dot_general(
        a, b, (((1,), (0,)), ((), ())), precision=HIGHEST, preferred_element_type=F32
    )


def dot_t(a, b):
    return lax.dot_general(
        a, b, (((1,), (1,)), ((), ())), precision=HIGHEST, preferred_element_type=F32
    )


def halves(a):
    high = a.astype(BF16)
    return high, (a - high.astype(F32)).astype(BF16)


def both(a):
    return jnp.concatenate(halves(a), axis=0)


def fold(out):
    n = out.shape[0] // 2
    return out[0:n] + out[n:]


def dot_w(a, w):
    n = w.shape[1] // 2
    out = fold(jnp.dot(both(a), w, preferred_element_type=F32))
    return out[:, 0:n] + out[:, n:]


def units():
    return {d: 5 - d.bit_length() for d in range(1, 16)}


def offsets(count):
    at, out = 0, {}
    for d in sorted(count):
        out[d] = at
        at += count[d]
    return out, at


def butterfly(values):
    while len(values) > 1:
        values = [values[i] + values[i + 1] for i in range(0, len(values), 2)]
    return values[0]


ORDER = (8, 15, 14, 13, 12, 11, 10, 9, 7, 6, 5, 4, 3, 2, 1)


def tile_rows(x):
    return jnp.concatenate([x, x], axis=0)


def shuffle(t):
    row = lax.broadcasted_iota(jnp.int32, t.shape, 0) % 4
    chunk = lax.broadcasted_iota(jnp.int32, t.shape, 1) // 32
    rows, lanes = t.shape
    out = t
    for delta in (-3, -2, -1, 1, 2, 3):
        moved = pltpu.roll(t, delta % rows, 0)
        moved = pltpu.roll(moved, (-32 * delta) % lanes, 1)
        out = jnp.where(row - chunk == delta, moved, out)
    return out


def kernel(
    rs_h, cond_h, linv_h, basis_h, e0_h, nt_h, f0_h, nf_h,
    sol_o, res_o, dir_o,
    rs, cond, linv, basis, e0, nt, f0, nf,
    pf, rf, basis2, linv2, pa, pb, ra, rb, gs, lb, wt, tmp,
    zs1, zb1, zs2, zb2, cs1, cb1, cs2, cb2, gs1, gb1, gs2, gb2,
    hrs, hrb, hcs, hcb, krs, krb, kcs, kcb,
    lsem, ssem, rsem, hsem, hrsem,
):
    X = lax.axis_index("gx")
    Z = lax.axis_index("gy")
    z_peer = lambda d: (X, Z ^ d)
    c_peer = (X ^ 1, Z)
    g_peer = lambda d: (X ^ (2 * d), Z)
    x_up, x_down = (X + 1) % 32, (X + 31) % 32
    z_up, z_down = (Z + 1) % 16, (Z + 15) % 16

    loads = {}
    parts = [
        ("e0", e0_h.at[0, 0], e0),
        ("nt0", nt_h.at[0, 0, pl.ds(0, 3)], nt.at[pl.ds(0, 3)]),
        ("rs", rs_h, rs),
    ]
    for i in range(4):
        at = pl.ds(4 * i, 4)
        parts.append(("basis%d" % i, basis_h.at[at], basis.at[at]))
    parts += [
        ("nt1", nt_h.at[0, 0, pl.ds(3, 5)], nt.at[pl.ds(3, 5)]),
        ("cond", cond_h, cond),
        ("nf", nf_h.at[0, 0], nf),
        ("linv", linv_h, linv),
        ("f0", f0_h.at[0, 0], f0),
    ]
    for i, (name, src, dst) in enumerate(parts):
        loads[name] = pltpu.make_async_copy(src, dst, lsem.at[i])
        loads[name].start()

    barrier = pltpu.get_barrier_semaphore()
    others = [z_peer(d) for d in ORDER] + [g_peer(d) for d in ORDER] + [c_peer]
    halo = [(x_up, Z), (x_down, Z), (X, z_up), (X, z_down)]
    for who in others + halo:
        pl.semaphore_signal(barrier, inc=1, device_id=who, device_id_type=MESH)

    def send(src, dst, sends, recvs, who):
        copy = pltpu.make_async_remote_copy(
            src_ref=src, dst_ref=dst, send_sem=sends, recv_sem=recvs,
            device_id=who, device_id_type=MESH,
        )
        copy.start()
        return copy

    def send_group(src, buf, slot, peer):
        count = units()
        at, _ = offsets(count)
        for d in ORDER:
            n = count[d]
            send(
                src.at[pl.ds(0, n)], buf.at[pl.ds(at[d], n)], ssem.at[slot], rsem.at[slot], peer(d)
            )

    def send_all(src, buf, slot, peer):
        for d in ORDER:
            send(src, buf.at[d - 1], ssem.at[slot], rsem.at[slot], peer(d))

    def wait_bytes(buf, sem):
        pltpu.make_async_copy(buf, buf, sem).wait()

    def group_sums(src, buf):
        count = units()
        at, _ = offsets(count)
        out = []
        for unit in range(4):
            reach = [d for d in range(1, 16) if count[d] > unit]
            out.append(butterfly([src[unit]] + [buf[at[d] + unit] for d in reach]))
        return out

    def all_sums(src, buf, unit, size):
        terms = [src[unit]] + [buf[d, unit] for d in range(15)]
        return [butterfly(terms[i : i + size]) for i in range(0, 16, size)]

    def products(src, buf, unit, other, size):
        sums = all_sums(src, buf, unit, size)
        images = all_sums(src, buf, other, size)
        return sums[0], butterfly([s * m for s, m in zip(sums, images)])

    row = lax.broadcasted_iota(jnp.int32, (32, K), 0)
    lane = lax.broadcasted_iota(jnp.int32, (32, K), 1)

    def send_edges(t, rows_src, rows_buf, cols_src, cols_buf, first):
        rows_src[0] = jnp.concatenate([t[15:16], t[31:32]], axis=0)
        rows_src[1] = jnp.concatenate([t[0:1], t[16:17]], axis=0)
        lane8 = lane[0:8]
        last_col = pltpu.roll(t[0:8], 1, 1)
        first_col = t[0:8]
        for j in range(1, 4):
            part = t[8 * j : 8 * j + 8]
            last_col = jnp.where(lane8 == j, pltpu.roll(part, j + 1, 1), last_col)
            first_col = jnp.where(lane8 == j, pltpu.roll(part, j, 1), first_col)
        cols_src[0] = last_col
        cols_src[1] = first_col
        return [
            send(rows_src.at[0], rows_buf.at[0], hsem.at[first], hrsem.at[first], (x_up, Z)),
            send(rows_src.at[1], rows_buf.at[1], hsem.at[first + 1], hrsem.at[first + 1], (x_down, Z)),
            send(cols_src.at[0], cols_buf.at[0], hsem.at[first + 2], hrsem.at[first + 2], (X, z_up)),
            send(cols_src.at[1], cols_buf.at[1], hsem.at[first + 3], hrsem.at[first + 3], (X, z_down)),
        ]

    def beside(t, rows_buf, cols_buf):
        def spread(h):
            return jnp.concatenate(
                [jnp.broadcast_to(h[0:1], (16, K)), jnp.broadcast_to(h[1:2], (16, K))], axis=0
            )

        low = spread(jnp.where(X > 0, rows_buf[0], 0.0))
        high = spread(jnp.where(X < 31, rows_buf[1], 0.0))
        left = jnp.where(Z > 0, cols_buf[0], 0.0)
        right = jnp.where(Z < 15, cols_buf[1], 0.0)
        left = jnp.concatenate([left] + [pltpu.roll(left, K - j, 1) for j in range(1, 4)], axis=0)
        right = jnp.concatenate([pltpu.roll(right, K - 1 - j, 1) for j in range(4)], axis=0)
        return (
            jnp.where(row % 16 == 15, high, pltpu.roll(t, 31, 0)),
            jnp.where(row % 16 == 0, low, pltpu.roll(t, 1, 0)),
            jnp.where(lane == K - 1, right, pltpu.roll(t, K - 1, 1)),
            jnp.where(lane == 0, left, pltpu.roll(t, 1, 1)),
        )

    def flat_rows(ref):
        return jnp.concatenate([ref[:, x, :] for x in range(16)], axis=1)

    def coefficients(ref):
        return dot_w(flat_rows(ref), basis2[...])

    def leaf_apply(t):
        high, low = halves(shuffle(t))
        high, low = high.astype(F32), low.astype(F32)
        for i in range(16):
            j = 16 + i
            lhs = jnp.concatenate(
                [high[i : i + 1], high[j : j + 1], low[i : i + 1], low[j : j + 1]], axis=0
            )
            out = fold(jnp.dot(lhs.astype(BF16), linv2[i], preferred_element_type=F32))
            out = out[:, 0:K] + out[:, K:]
            tmp[pl.ds(i, 1)] = out[0:1]
            tmp[pl.ds(j, 1)] = out[1:2]
        return shuffle(tmp[...])

    def spread_out(y):
        lhs = both(y)
        w = fold(
            lax.dot_general(
                jnp.concatenate([lhs, lhs], axis=1), basis2[...],
                (((1,), (1,)), ((), ())), preferred_element_type=F32,
            )
        )
        for x in range(16):
            wt[:, x, :] = w[:, x * K : (x + 1) * K]
        return wt[...].reshape(32, K)

    def keep(ref, count, i, matrix):
        high, low = halves(matrix)
        ref[:, i * K : (i + 1) * K] = high
        ref[:, (count + i) * K : (count + i + 1) * K] = low

    def keep_down(h, matrix):
        high, low = halves(matrix)
        gs[h * K : (h + 1) * K, 0:K] = high
        gs[h * K : (h + 1) * K, K:] = low

    def put(ref, rows2, first=0):
        for i in range(rows2.shape[1] // K):
            ref[first + i] = rows2[:, i * K : (i + 1) * K]

    loads["e0"].wait()
    loads["nt0"].wait()
    p = e0[...]
    pf[0] = p
    keep(pa, 4, 3, p)
    for i in range(3):
        p = dot(p, nt[i])
        pf[i + 1] = p
        keep(pa, 4, 2 - i, p)
    loads["rs"].wait()
    for i in range(4):
        loads["basis%d" % i].wait()
        high, low = halves(basis[pl.ds(4 * i, 4)].reshape(4 * K, K))
        basis2[4 * K * i : 4 * K * (i + 1), 0:K] = high
        basis2[4 * K * i : 4 * K * (i + 1), K:] = low
    u0 = coefficients(rs)
    put(zs1, dot_w(u0, pa[...]))
    pl.semaphore_wait(barrier, len(others) + len(halo))
    send_group(zs1, zb1, 0, z_peer)

    loads["cond"].wait()
    k32 = tile_rows(cond[...])
    edges_k = send_edges(k32, krs, krb, kcs, kcb, 0)
    loads["nt1"].wait()
    r = nt[3]
    rf[0] = r
    keep(ra, 5, 4, r)
    for i in range(4):
        r = dot(r, nt[4 + i])
        rf[i + 1] = r
        keep(ra, 5, 3 - i, r)
    loads["linv"].wait()
    for i in range(16):
        high, low = halves(linv[i // 4, i % 4])
        linv2[i, :, 0:K] = high
        linv2[i, :, K:] = low
    b32 = rs[...].reshape(32, K)
    lb[...] = leaf_apply(b32)
    loads["nf"].wait()
    loads["f0"].wait()
    keep_down(0, f0[...])
    for h in range(1, 5):
        keep_down(h, dot_t(nf[h - 1], pf[h - 1]))

    wait_bytes(zb1, rsem.at[0])
    u4, u3, u2, u1 = group_sums(zs1, zb1)
    put(cs1, dot_w(u4, ra[...]))
    core1 = send(cs1, cb1, ssem.at[1], rsem.at[1], c_peer)
    for h in range(6, 8):
        keep_down(h, dot_t(dot_t(nf[h - 1], rf[h - 5]), pf[3]))
    core1.wait_recv()
    u5 = cs1[4] + cb1[4]
    gs1[...] = cs1[pl.ds(0, 4)] + cb1[pl.ds(0, 4)]
    send_group(gs1, gb1, 2, g_peer)
    for h in (5, 8, 9):
        keep_down(h, dot_t(dot_t(nf[h - 1], rf[h - 5]), pf[3]))
    y = dot_w(jnp.concatenate([u0, u1, u2, u3, u4, u5], axis=1), gs[0 : 6 * K])
    for e in edges_k:
        e.wait_recv()
    weights = [0.5 * (k32 + other) for other in beside(k32, krb, kcb)]
    wait_bytes(gb1, rsem.at[2])
    u9, u8, u7, u6 = group_sums(gs1, gb1)
    y = y + dot_w(jnp.concatenate([u6, u7, u8, u9], axis=1), gs[6 * K : 10 * K])
    z = lb[...] + spread_out(y)

    edges_z = send_edges(z, hrs, hrb, hcs, hcb, 4)
    for h in range(1, 4):
        keep(pb, 4, 3 - h, dot(pf[h - 1], nf[h - 1]))
    keep(pb, 4, 3, f0[...])
    for h in range(5, 10):
        keep(rb, 6, 9 - h, dot(rf[h - 5], nf[h - 1]))
    keep(rb, 6, 5, nf[3])
    for e in edges_z:
        e.wait_recv()
    applied = jnp.zeros_like(z)
    for weight, other in zip(weights, beside(z, hrb, hcb)):
        applied = applied + weight * (z - other)
    res_o[...] = applied.reshape(2, 16, K)

    lane2 = lane[0:2]

    def columns(t):
        return jnp.sum(t.reshape(2, 16, K), axis=1)

    def quadratic(t):
        return jnp.where(lane2 >= 64, t + pltpu.roll(t, 64, 1), 0.0)

    u0 = coefficients(res_o)
    put(zs2, dot_w(u0, pa[...]), 1)
    low = dot_w(u0, pb[...])
    put(zs2, low[:, 0 : 3 * K], 5)
    near = leaf_apply(applied)
    inner = jnp.concatenate([columns(b32 * z), columns(z * applied)], axis=0)
    inner = inner + pltpu.roll(inner, 64, 1)
    inner = inner + pltpu.roll(inner, 32, 1)
    zs2[0] = jnp.where(lane2 < 32, inner[0:2], jnp.where(lane2 < 64, inner[2:4], 0.0)) + quadratic(
        columns(applied * near) + u0 * low[:, 3 * K :]
    )
    send_all(zs2, zb2, 3, z_peer)
    wait_bytes(zb2, rsem.at[3])
    u4 = all_sums(zs2, zb2, 1, 16)[0]
    up = dot_w(u4, ra[...])
    image = dot_w(u4, rb[...])
    u3, q3 = products(zs2, zb2, 2, 5, 8)
    u2, q2 = products(zs2, zb2, 3, 6, 4)
    u1, q1 = products(zs2, zb2, 4, 7, 2)
    cs2[0] = all_sums(zs2, zb2, 0, 16)[0] + quadratic(q1 + q2 + q3 + u4 * image[:, 5 * K :])
    put(cs2, up[:, 0 : 4 * K], 1)
    put(cs2, image[:, 0 : 4 * K], 5)
    cs2[9] = up[:, 4 * K :]
    cs2[10] = image[:, 4 * K : 5 * K]
    core2 = send(cs2, cb2, ssem.at[4], rsem.at[4], c_peer)
    core2.wait_recv()
    u5 = cs2[9] + cb2[9]
    gs2[...] = cs2[pl.ds(0, 9)] + cb2[pl.ds(0, 9)]
    gs2[0] = gs2[0] + quadratic(u5 * (cs2[10] + cb2[10]))
    send_all(gs2, gb2, 5, g_peer)
    y = dot_w(jnp.concatenate([u0, u1, u2, u3, u4, u5], axis=1), gs[0 : 6 * K])
    wait_bytes(gb2, rsem.at[5])
    u9, q9 = products(gs2, gb2, 1, 5, 16)
    u8, q8 = products(gs2, gb2, 2, 6, 8)
    u7, q7 = products(gs2, gb2, 3, 7, 4)
    u6, q6 = products(gs2, gb2, 4, 8, 2)
    y = y + dot_w(jnp.concatenate([u6, u7, u8, u9], axis=1), gs[6 * K : 10 * K])
    mapped = near + spread_out(y)
    inner = all_sums(gs2, gb2, 0, 16)[0] + quadratic(q6 + q7 + q8 + q9)

    def over_lanes(t):
        return jnp.sum(t, axis=1, keepdims=True)

    rz_old = over_lanes(jnp.where(lane2 < 32, inner, 0.0))
    curvature = over_lanes(jnp.where((lane2 >= 32) & (lane2 < 64), inner, 0.0))
    squared = over_lanes(jnp.where(lane2 >= 64, inner, 0.0))
    step = rz_old / curvature
    rz_new = rz_old - 2.0 * step * curvature + step * step * squared

    def over_tile(t):
        return jnp.concatenate(
            [jnp.broadcast_to(t[0:1], (16, K)), jnp.broadcast_to(t[1:2], (16, K))], axis=0
        )

    step32 = over_tile(step)
    sol_o[...] = (step32 * z).reshape(2, 16, K)
    res_o[...] = (b32 - step32 * applied).reshape(2, 16, K)
    second = z - step32 * mapped
    dir_o[...] = (second + over_tile(rz_new / rz_old) * z).reshape(2, 16, K)

    for e in edges_k + edges_z + [core1, core2]:
        e.wait_send()
    for buf, slot in ((zb1, 0), (gb1, 2), (zb2, 3), (gb2, 5)):
        wait_bytes(buf, ssem.at[slot])


def on_device(*args):
    unit = lambda *n: pltpu.VMEM(n + (2, K), F32)
    square = lambda *n: pltpu.VMEM(n + (K, K), F32)
    out = jax.ShapeDtypeStruct((2, 16, K), F32)
    return pl.pallas_call(
        kernel,
        name="pcg_step",
        out_shape=(out, out, out),
        in_specs=[pl.BlockSpec(memory_space=pl.ANY)] * 8,
        out_specs=[pl.BlockSpec(memory_space=pltpu.VMEM)] * 3,
        scratch_shapes=[
            pltpu.VMEM((2, 16, K), F32), pltpu.VMEM((16, K), F32), square(4, 4), square(16),
            square(), square(8), square(), square(9),
            square(4), square(5), pltpu.VMEM((16 * K, 2 * K), BF16), pltpu.VMEM((16, K, 2 * K), BF16),
            pltpu.VMEM((K, 8 * K), BF16), pltpu.VMEM((K, 8 * K), BF16),
            pltpu.VMEM((K, 10 * K), BF16), pltpu.VMEM((K, 12 * K), BF16),
            pltpu.VMEM((10 * K, 2 * K), BF16),
            pltpu.VMEM((32, K), F32), pltpu.VMEM((2, 16, K), F32), pltpu.VMEM((32, K), F32),
            unit(4), unit(26), unit(8), unit(15, 8), unit(5), unit(5), unit(11), unit(11),
            unit(4), unit(26), unit(9), unit(15, 9),
            unit(2), unit(2), pltpu.VMEM((2, 8, K), F32), pltpu.VMEM((2, 8, K), F32),
            unit(2), unit(2), pltpu.VMEM((2, 8, K), F32), pltpu.VMEM((2, 8, K), F32),
            pltpu.SemaphoreType.DMA((12,)), pltpu.SemaphoreType.DMA((6,)),
            pltpu.SemaphoreType.DMA((6,)), pltpu.SemaphoreType.DMA((8,)),
            pltpu.SemaphoreType.DMA((8,)),
        ],
        compiler_params=pltpu.CompilerParams(
            collective_id=0, has_side_effects=True, vmem_limit_bytes=60 * 1024 * 1024
        ),
    )(*args)


def solution(mesh):
    return jax.shard_map(
        on_device,
        mesh=mesh,
        in_specs=(
            P(None, "gx", "gy"),
            P("gx", "gy"),
            P("gx", "gy", None, None),
            P("gx", "gy", None),
            P("gx", "gy", None, None),
            P("gx", "gy", None, None, None),
            P("gx", "gy", None, None),
            P("gx", "gy", None, None, None),
        ),
        out_specs=(P(None, "gx", "gy"), P(None, "gx", "gy"), P(None, "gx", "gy")),
        check_vma=False,
    )
```

time: 64.5 us -> 54.8 us (0.85); the launches traced: 64.2 us -> 53.7 us
  Pallas kernels: 60.9 us -> 50.4 us
    pallas_call x1, Pallas kernels: 60.9 us -> 50.4 us  [on_device(): pl.pallas_call(kernel, name='pcg_step', out_shape=(out, out, out), in_spe...]
where the time goes in v2:
time: 54.8 us; the launch traced here: 53.7 us
  Pallas kernels  50.4 us (92%)
  local copies, waits for them, and re-layouts  2.66 us (5%)
  between operations  0.65 us (1%)
    pallas_call x1, Pallas kernels, on_device(): pl.pallas_call(kernel, name='pcg_step', out_shape=(out, out, out), in_spe...  50.4 us
    unnamed x7, local copies, waits for them, and re-layouts  2.66 us

profile of v2, /device:TPU:1, one launch (start us, length us, event | category | flops | bytes accessed | tf_op | source)
XLA Modules:
  0.0 53.7 jit_solution(5749615777363410291)
XLA Ops:
  0.6 50.4 %pcg_step.1 = (f32[2,16,128]{2,1,0:T(8,128)}, f32[2,16,128]{2,1,0:T(8,128)}, f32[2,16,128]{2,1,0:T(8,128)}) custom-call(f32[2,16,128]{2,1,0:T(8,128)} %rs_h.1, f32[16,128]{1,0:T(8,128)} %cond_h.1, f32[4,4,128,128]{3,2,1,0:T(8,128)} %linv_h.1, f32[16,128,128]{2,1,0:T(8,128)} %basis_h.1, f32[1,1,128,128]{3,2,1,0:T(8,128)} %e0_h.1, ...), custom_call_target="tpu_custom_call" | custom-call | tf_op jit(solution)/shard_map/pcg_step/pallas_call | solution.py:413
  51.0 0.0 copy-start.1
  51.1 1.3 %copy.14 = f32[2,16,128]{2,1,0:T(8,128)} copy(f32[2,16,128]{2,1,0:T(8,128)} %get-tuple-element.6) | data formatting | bytes 32768
  52.4 0.0 copy-done.1
  52.4 0.0 copy-start
  52.4 0.6 %copy.15 = f32[2,16,128]{2,1,0:T(8,128)} copy(f32[2,16,128]{2,1,0:T(8,128)S(1)} %copy-done.1) | data formatting | bytes 32768
  53.0 0.1 copy-done
  53.1 0.6 %copy.16 = f32[2,16,128]{2,1,0:T(8,128)} copy(f32[2,16,128]{2,1,0:T(8,128)S(1)} %copy-done) | data formatting | bytes 32768
Async XLA Ops:
  51.0 1.3 %copy-start.1 = (f32[2,16,128]{2,1,0:T(8,128)S(1)}, f32[2,16,128]{2,1,0:T(8,128)}, u32[]{:S(2)}) copy-start(f32[2,16,128]{2,1,0:T(8,128)} %get-tuple-element.7) | copy-start | bytes 49156
  52.4 0.7 %copy-start = (f32[2,16,128]{2,1,0:T(8,128)S(1)}, f32[2,16,128]{2,1,0:T(8,128)}, u32[]{:S(2)}) copy-start(f32[2,16,128]{2,1,0:T(8,128)} %get-tuple-element.8) | copy-start | bytes 49156

commit v3 on v2

--- a/solution.py
+++ b/solution.py
@@ -83,7 +83,7 @@
 
 def kernel(
     rs_h, cond_h, linv_h, basis_h, e0_h, nt_h, f0_h, nf_h,
-    sol_o, res_o, dir_o,
+    out_o,
     rs, cond, linv, basis, e0, nt, f0, nf,
     pf, rf, basis2, linv2, pa, pb, ra, rb, gs, lb, wt, tmp,
     zs1, zb1, zs2, zb2, cs1, cb1, cs2, cb2, gs1, gb1, gs2, gb2,
@@ -97,6 +97,12 @@
     g_peer = lambda d: (X ^ (2 * d), Z)
     x_up, x_down = (X + 1) % 32, (X + 31) % 32
     z_up, z_down = (Z + 1) % 16, (Z + 15) % 16
+
+    barrier = pltpu.get_barrier_semaphore()
+    others = [z_peer(d) for d in ORDER] + [g_peer(d) for d in ORDER] + [c_peer]
+    others.append(((X + 31 + 2 * (X % 2)) % 32, Z))
+    for who in others:
+        pl.semaphore_signal(barrier, inc=1, device_id=who, device_id_type=MESH)
 
     loads = {}
     parts = [
@@ -118,12 +124,6 @@
         loads[name] = pltpu.make_async_copy(src, dst, lsem.at[i])
         loads[name].start()
 
-    barrier = pltpu.get_barrier_semaphore()
-    others = [z_peer(d) for d in ORDER] + [g_peer(d) for d in ORDER] + [c_peer]
-    halo = [(x_up, Z), (x_down, Z), (X, z_up), (X, z_down)]
-    for who in others + halo:
-        pl.semaphore_signal(barrier, inc=1, device_id=who, device_id_type=MESH)
-
     def send(src, dst, sends, recvs, who):
         copy = pltpu.make_async_remote_copy(
             src_ref=src, dst_ref=dst, send_sem=sends, recv_sem=recvs,
@@ -270,12 +270,6 @@
         basis2[4 * K * i : 4 * K * (i + 1), K:] = low
     u0 = coefficients(rs)
     put(zs1, dot_w(u0, pa[...]))
-    pl.semaphore_wait(barrier, len(others) + len(halo))
-    send_group(zs1, zb1, 0, z_peer)
-
-    loads["cond"].wait()
-    k32 = tile_rows(cond[...])
-    edges_k = send_edges(k32, krs, krb, kcs, kcb, 0)
     loads["nt1"].wait()
     r = nt[3]
     rf[0] = r
@@ -284,6 +278,12 @@
         r = dot(r, nt[4 + i])
         rf[i + 1] = r
         keep(ra, 5, 3 - i, r)
+    pl.semaphore_wait(barrier, len(others))
+    send_group(zs1, zb1, 0, z_peer)
+
+    loads["cond"].wait()
+    k32 = tile_rows(cond[...])
+    edges_k = send_edges(k32, krs, krb, kcs, kcb, 0)
     loads["linv"].wait()
     for i in range(16):
         high, low = halves(linv[i // 4, i % 4])
@@ -296,19 +296,23 @@
     keep_down(0, f0[...])
     for h in range(1, 5):
         keep_down(h, dot_t(nf[h - 1], pf[h - 1]))
+    for h in range(5, 10):
+        keep_down(h, dot_t(dot_t(nf[h - 1], rf[h - 5]), pf[3]))
 
     wait_bytes(zb1, rsem.at[0])
     u4, u3, u2, u1 = group_sums(zs1, zb1)
     put(cs1, dot_w(u4, ra[...]))
     core1 = send(cs1, cb1, ssem.at[1], rsem.at[1], c_peer)
-    for h in range(6, 8):
-        keep_down(h, dot_t(dot_t(nf[h - 1], rf[h - 5]), pf[3]))
     core1.wait_recv()
     u5 = cs1[4] + cb1[4]
     gs1[...] = cs1[pl.ds(0, 4)] + cb1[pl.ds(0, 4)]
     send_group(gs1, gb1, 2, g_peer)
-    for h in (5, 8, 9):
-        keep_down(h, dot_t(dot_t(nf[h - 1], rf[h - 5]), pf[3]))
+    for h in range(1, 4):
+        keep(pb, 4, 3 - h, dot(pf[h - 1], nf[h - 1]))
+    keep(pb, 4, 3, f0[...])
+    for h in range(5, 10):
+        keep(rb, 6, 9 - h, dot(rf[h - 5], nf[h - 1]))
+    keep(rb, 6, 5, nf[3])
     y = dot_w(jnp.concatenate([u0, u1, u2, u3, u4, u5], axis=1), gs[0 : 6 * K])
     for e in edges_k:
         e.wait_recv()
@@ -319,18 +323,12 @@
     z = lb[...] + spread_out(y)
 
     edges_z = send_edges(z, hrs, hrb, hcs, hcb, 4)
-    for h in range(1, 4):
-        keep(pb, 4, 3 - h, dot(pf[h - 1], nf[h - 1]))
-    keep(pb, 4, 3, f0[...])
-    for h in range(5, 10):
-        keep(rb, 6, 9 - h, dot(rf[h - 5], nf[h - 1]))
-    keep(rb, 6, 5, nf[3])
     for e in edges_z:
         e.wait_recv()
     applied = jnp.zeros_like(z)
     for weight, other in zip(weights, beside(z, hrb, hcb)):
         applied = applied + weight * (z - other)
-    res_o[...] = applied.reshape(2, 16, K)
+    wt[...] = applied.reshape(2, 16, K)
 
     lane2 = lane[0:2]
 
@@ -340,7 +338,7 @@
     def quadratic(t):
         return jnp.where(lane2 >= 64, t + pltpu.roll(t, 64, 1), 0.0)
 
-    u0 = coefficients(res_o)
+    u0 = coefficients(wt)
     put(zs2, dot_w(u0, pa[...]), 1)
     low = dot_w(u0, pb[...])
     put(zs2, low[:, 0 : 3 * K], 5)
@@ -395,10 +393,10 @@
         )
 
     step32 = over_tile(step)
-    sol_o[...] = (step32 * z).reshape(2, 16, K)
-    res_o[...] = (b32 - step32 * applied).reshape(2, 16, K)
+    out_o[0:2] = (step32 * z).reshape(2, 16, K)
+    out_o[2:4] = (b32 - step32 * applied).reshape(2, 16, K)
     second = z - step32 * mapped
-    dir_o[...] = (second + over_tile(rz_new / rz_old) * z).reshape(2, 16, K)
+    out_o[4:6] = (second + over_tile(rz_new / rz_old) * z).reshape(2, 16, K)
 
     for e in edges_k + edges_z + [core1, core2]:
         e.wait_send()
@@ -409,13 +407,12 @@
 def on_device(*args):
     unit = lambda *n: pltpu.VMEM(n + (2, K), F32)
     square = lambda *n: pltpu.VMEM(n + (K, K), F32)
-    out = jax.ShapeDtypeStruct((2, 16, K), F32)
-    return pl.pallas_call(
+    out = pl.pallas_call(
         kernel,
         name="pcg_step",
-        out_shape=(out, out, out),
+        out_shape=jax.ShapeDtypeStruct((6, 16, K), F32),
         in_specs=[pl.BlockSpec(memory_space=pl.ANY)] * 8,
-        out_specs=[pl.BlockSpec(memory_space=pltpu.VMEM)] * 3,
+        out_specs=pl.BlockSpec(memory_space=pltpu.VMEM),
         scratch_shapes=[
             pltpu.VMEM((2, 16, K), F32), pltpu.VMEM((16, K), F32), square(4, 4), square(16),
             square(), square(8), square(), square(9),
@@ -436,6 +433,7 @@
             collective_id=0, has_side_effects=True, vmem_limit_bytes=60 * 1024 * 1024
         ),
     )(*args)
+    return out[0:2], out[2:4], out[4:6]
 
 
 def solution(mesh):

time: 54.8 us -> 52.5 us (0.958)
  local copies, waits for them, and re-layouts: 2.66 us -> 1.37 us
  Pallas kernels: 50.4 us -> 49.5 us
    unnamed x7 -> x0, local copies, waits for them, and re-layouts: 2.66 us -> none
    slice x0 -> x1, local copies, waits for them, and re-layouts: none -> 1.37 us  [on_device(): return (out[0:2], out[2:4], out[4:6])]
    pallas_call x1, Pallas kernels: 50.4 us -> 49.5 us  [on_device(): pl.pallas_call(kernel, name='pcg_step', out_shape=jax.ShapeDtypeStruct((6...]
where the time goes in v3:
time: 52.5 us; the launch traced here: 51.5 us
  Pallas kernels  49.5 us (94%)
  local copies, waits for them, and re-layouts  1.37 us (3%)
  between operations  0.64 us (1%)
    pallas_call x1, Pallas kernels, on_device(): pl.pallas_call(kernel, name='pcg_step', out_shape=jax.ShapeDtypeStruct((6...  49.5 us
    slice x1, local copies, waits for them, and re-layouts, on_device(): return (out[0:2], out[2:4], out[4:6])  1.37 us

profile of v3, /device:TPU:1, one launch (start us, length us, event | category | flops | bytes accessed | tf_op | source)
XLA Modules:
  0.0 51.5 jit_solution(2208375251784993464)
XLA Ops:
  0.6 49.5 %pcg_step.1 = f32[6,16,128]{2,1,0:T(8,128)} custom-call(f32[2,16,128]{2,1,0:T(8,128)} %rs_h.1, f32[16,128]{1,0:T(8,128)} %cond_h.1, f32[4,4,128,128]{3,2,1,0:T(8,128)} %linv_h.1, f32[16,128,128]{2,1,0:T(8,128)} %basis_h.1, f32[1,1,128,128]{3,2,1,0:T(8,128)} %e0_h.1, f32[1,1,8,128,128]{4,3,2,1,0:T(8,128)} %nt_h.1, f32[1,1,128,128]{3,2,1,0:T(8,128)} %f0_h.1, ...), custom_call_target="tpu_custom_call" | custom-call | tf_op jit(solution)/shard_map/pcg_step/pallas_call | solution.py:410
  50.1 1.4 %fusion = (f32[2,16,128]{2,1,0:T(8,128)}, f32[2,16,128]{2,1,0:T(8,128)}, f32[2,16,128]{2,1,0:T(8,128)}) fusion(f32[6,16,128]{2,1,0:T(8,128)} %pcg_step.1), kind=kLoop, calls=%fused_computation | loop fusion | bytes 98304 | tf_op jit(solution)/shard_map/slice | solution.py:436

commit v4 on v3

--- a/solution.py
+++ b/solution.py
@@ -88,19 +88,21 @@
     pf, rf, basis2, linv2, pa, pb, ra, rb, gs, lb, wt, tmp,
     zs1, zb1, zs2, zb2, cs1, cb1, cs2, cb2, gs1, gb1, gs2, gb2,
     hrs, hrb, hcs, hcb, krs, krb, kcs, kcb,
-    lsem, ssem, rsem, hsem, hrsem,
+    hxs, hxb, hx2, hzs, hzb, hz2,
+    lsem, ssem, rsem, hsem, hrsem, msem, mrsem,
 ):
     X = lax.axis_index("gx")
     Z = lax.axis_index("gy")
     z_peer = lambda d: (X, Z ^ d)
     c_peer = (X ^ 1, Z)
     g_peer = lambda d: (X ^ (2 * d), Z)
-    x_up, x_down = (X + 1) % 32, (X + 31) % 32
+    even = X % 2 == 0
+    beyond = (X + 31 + 2 * (X % 2)) % 32
     z_up, z_down = (Z + 1) % 16, (Z + 15) % 16
 
     barrier = pltpu.get_barrier_semaphore()
     others = [z_peer(d) for d in ORDER] + [g_peer(d) for d in ORDER] + [c_peer]
-    others.append(((X + 31 + 2 * (X % 2)) % 32, Z))
+    others.append((beyond, Z))
     for who in others:
         pl.semaphore_signal(barrier, inc=1, device_id=who, device_id_type=MESH)
 
@@ -170,8 +172,10 @@
     lane = lax.broadcasted_iota(jnp.int32, (32, K), 1)
 
     def send_edges(t, rows_src, rows_buf, cols_src, cols_buf, first):
-        rows_src[0] = jnp.concatenate([t[15:16], t[31:32]], axis=0)
-        rows_src[1] = jnp.concatenate([t[0:1], t[16:17]], axis=0)
+        first_row = jnp.concatenate([t[0:1], t[16:17]], axis=0)
+        last_row = jnp.concatenate([t[15:16], t[31:32]], axis=0)
+        rows_src[0] = jnp.where(even, last_row, first_row)
+        rows_src[1] = jnp.where(even, first_row, last_row)
         lane8 = lane[0:8]
         last_col = pltpu.roll(t[0:8], 1, 1)
         first_col = t[0:8]
@@ -182,24 +186,30 @@
         cols_src[0] = last_col
         cols_src[1] = first_col
         return [
-            send(rows_src.at[0], rows_buf.at[0], hsem.at[first], hrsem.at[first], (x_up, Z)),
-            send(rows_src.at[1], rows_buf.at[1], hsem.at[first + 1], hrsem.at[first + 1], (x_down, Z)),
+            send(rows_src.at[0], rows_buf.at[0], hsem.at[first], hrsem.at[first], c_peer),
+            send(rows_src.at[1], rows_buf.at[1], hsem.at[first + 1], hrsem.at[first + 1], (beyond, Z)),
             send(cols_src.at[0], cols_buf.at[0], hsem.at[first + 2], hrsem.at[first + 2], (X, z_up)),
             send(cols_src.at[1], cols_buf.at[1], hsem.at[first + 3], hrsem.at[first + 3], (X, z_down)),
         ]
 
-    def beside(t, rows_buf, cols_buf):
+    def beside(t, rows_buf, cols_buf, late=None):
         def spread(h):
             return jnp.concatenate(
                 [jnp.broadcast_to(h[0:1], (16, K)), jnp.broadcast_to(h[1:2], (16, K))], axis=0
             )
 
-        low = spread(jnp.where(X > 0, rows_buf[0], 0.0))
-        high = spread(jnp.where(X < 31, rows_buf[1], 0.0))
-        left = jnp.where(Z > 0, cols_buf[0], 0.0)
-        right = jnp.where(Z < 15, cols_buf[1], 0.0)
+        inside, outside = rows_buf[0], rows_buf[1]
+        if late is not None:
+            inside, outside = inside + late[0], outside + late[1]
+        low = spread(jnp.where(X > 0, jnp.where(even, outside, inside), 0.0))
+        high = spread(jnp.where(X < 31, jnp.where(even, inside, outside), 0.0))
+        left, right = cols_buf[0], cols_buf[1]
         left = jnp.concatenate([left] + [pltpu.roll(left, K - j, 1) for j in range(1, 4)], axis=0)
         right = jnp.concatenate([pltpu.roll(right, K - 1 - j, 1) for j in range(4)], axis=0)
+        if late is not None:
+            left, right = left + late[2], right + late[3]
+        left = jnp.where(Z > 0, left, 0.0)
+        right = jnp.where(Z < 15, right, 0.0)
         return (
             jnp.where(row % 16 == 15, high, pltpu.roll(t, 31, 0)),
             jnp.where(row % 16 == 0, low, pltpu.roll(t, 1, 0)),
@@ -278,9 +288,35 @@
         r = dot(r, nt[4 + i])
         rf[i + 1] = r
         keep(ra, 5, 3 - i, r)
+    loads["nf"].wait()
+
+    def image(h):
+        return dot_t(dot_t(nf[h - 1], rf[h - 5]), pf[3])
+
+    images = {h: image(h) for h in (6, 7, 8)}
     pl.semaphore_wait(barrier, len(others))
     send_group(zs1, zb1, 0, z_peer)
 
+    images[9] = image(9)
+    edge_rows = jnp.concatenate(
+        [jnp.where(even, basis[15], basis[0]), jnp.where(even, basis[0], basis[15])], axis=0
+    )
+    edge_cols = jnp.concatenate([basis[:, K - 1, :], basis[:, 0, :]], axis=0)
+    for h in range(6, 10):
+        at = (h - 6) * K
+        keep_down(h, images[h])
+        of_rows = dot_t(images[h], edge_rows)
+        hxs[0, at : at + K] = of_rows[:, 0:K]
+        hxs[1, at : at + K] = of_rows[:, K:]
+        of_cols = dot_t(edge_cols, images[h])
+        hzs[0, :, at : at + K] = of_cols[0:16]
+        hzs[1, :, at : at + K] = of_cols[16:]
+    matrices = [
+        send(hxs.at[0], hxb.at[0], msem.at[0], mrsem.at[0], c_peer),
+        send(hxs.at[1], hxb.at[1], msem.at[1], mrsem.at[1], (beyond, Z)),
+        send(hzs.at[0], hzb.at[0], msem.at[2], mrsem.at[2], (X, z_up)),
+        send(hzs.at[1], hzb.at[1], msem.at[3], mrsem.at[3], (X, z_down)),
+    ]
     loads["cond"].wait()
     k32 = tile_rows(cond[...])
     edges_k = send_edges(k32, krs, krb, kcs, kcb, 0)
@@ -291,13 +327,11 @@
         linv2[i, :, K:] = low
     b32 = rs[...].reshape(32, K)
     lb[...] = leaf_apply(b32)
-    loads["nf"].wait()
     loads["f0"].wait()
     keep_down(0, f0[...])
     for h in range(1, 5):
         keep_down(h, dot_t(nf[h - 1], pf[h - 1]))
-    for h in range(5, 10):
-        keep_down(h, dot_t(dot_t(nf[h - 1], rf[h - 5]), pf[3]))
+    keep_down(5, image(5))
 
     wait_bytes(zb1, rsem.at[0])
     u4, u3, u2, u1 = group_sums(zs1, zb1)
@@ -306,27 +340,58 @@
     core1.wait_recv()
     u5 = cs1[4] + cb1[4]
     gs1[...] = cs1[pl.ds(0, 4)] + cb1[pl.ds(0, 4)]
-    send_group(gs1, gb1, 2, g_peer)
+    send_all(gs1, gb1, 2, g_peer)
+    y = dot_w(jnp.concatenate([u0, u1, u2, u3, u4, u5], axis=1), gs[0 : 6 * K])
+    z = lb[...] + spread_out(y)
+    edges_z = send_edges(z, hrs, hrb, hcs, hcb, 4)
     for h in range(1, 4):
         keep(pb, 4, 3 - h, dot(pf[h - 1], nf[h - 1]))
     keep(pb, 4, 3, f0[...])
     for h in range(5, 10):
         keep(rb, 6, 9 - h, dot(rf[h - 5], nf[h - 1]))
     keep(rb, 6, 5, nf[3])
-    y = dot_w(jnp.concatenate([u0, u1, u2, u3, u4, u5], axis=1), gs[0 : 6 * K])
     for e in edges_k:
         e.wait_recv()
     weights = [0.5 * (k32 + other) for other in beside(k32, krb, kcb)]
-    wait_bytes(gb1, rsem.at[2])
-    u9, u8, u7, u6 = group_sums(gs1, gb1)
-    y = y + dot_w(jnp.concatenate([u6, u7, u8, u9], axis=1), gs[6 * K : 10 * K])
-    z = lb[...] + spread_out(y)
-
-    edges_z = send_edges(z, hrs, hrb, hcs, hcb, 4)
+    for m in matrices:
+        m.wait_recv()
+    for side in range(2):
+        high, low = halves(hxb[side])
+        hx2[side, :, 0:K] = high
+        hx2[side, :, K:] = low
+        high, low = halves(hzb[side])
+        hz2[16 * side : 16 * side + 16] = high
+        hz2[32 + 16 * side : 48 + 16 * side] = low
     for e in edges_z:
         e.wait_recv()
+    wait_bytes(gb1, rsem.at[2])
+    u9 = all_sums(gs1, gb1, 0, 16)[0]
+    all8, all7, all6 = [all_sums(gs1, gb1, 4 - n, 2**n) for n in (3, 2, 1)]
+    mine = jnp.concatenate([all6[0], all7[0], all8[0], u9], axis=1)
+    apart = (X // 2) ^ (beyond // 2)
+    theirs6 = jnp.where(
+        apart == 15, all6[7], jnp.where(apart == 7, all6[3], jnp.where(apart == 3, all6[1], all6[0]))
+    )
+    theirs7 = jnp.where(apart == 15, all7[3], jnp.where(apart == 7, all7[1], all7[0]))
+    theirs8 = jnp.where(apart == 15, all8[1], all8[0])
+    theirs = jnp.concatenate([theirs6, theirs7, theirs8, u9], axis=1)
+    z = z + spread_out(dot_w(mine, gs[6 * K : 10 * K]))
+    cols = fold(
+        lax.dot_general(
+            hz2[...], both(mine), (((1,), (1,)), ((), ())), preferred_element_type=F32
+        )
+    )
+    cols = cols[:, 0:2] + cols[:, 2:4]
+
+    def column(side):
+        part = cols[16 * side : 16 * side + 16]
+        return jnp.concatenate(
+            [jnp.broadcast_to(part[:, i : i + 1], (16, K)) for i in range(2)], axis=0
+        )
+
+    late = (dot_w(mine, hx2[0]), dot_w(theirs, hx2[1]), column(0), column(1))
     applied = jnp.zeros_like(z)
-    for weight, other in zip(weights, beside(z, hrb, hcb)):
+    for weight, other in zip(weights, beside(z, hrb, hcb, late)):
         applied = applied + weight * (z - other)
     wt[...] = applied.reshape(2, 16, K)
 
@@ -353,15 +418,15 @@
     wait_bytes(zb2, rsem.at[3])
     u4 = all_sums(zs2, zb2, 1, 16)[0]
     up = dot_w(u4, ra[...])
-    image = dot_w(u4, rb[...])
+    mapped_up = dot_w(u4, rb[...])
     u3, q3 = products(zs2, zb2, 2, 5, 8)
     u2, q2 = products(zs2, zb2, 3, 6, 4)
     u1, q1 = products(zs2, zb2, 4, 7, 2)
-    cs2[0] = all_sums(zs2, zb2, 0, 16)[0] + quadratic(q1 + q2 + q3 + u4 * image[:, 5 * K :])
+    cs2[0] = all_sums(zs2, zb2, 0, 16)[0] + quadratic(q1 + q2 + q3 + u4 * mapped_up[:, 5 * K :])
     put(cs2, up[:, 0 : 4 * K], 1)
-    put(cs2, image[:, 0 : 4 * K], 5)
+    put(cs2, mapped_up[:, 0 : 4 * K], 5)
     cs2[9] = up[:, 4 * K :]
-    cs2[10] = image[:, 4 * K : 5 * K]
+    cs2[10] = mapped_up[:, 4 * K : 5 * K]
     core2 = send(cs2, cb2, ssem.at[4], rsem.at[4], c_peer)
     core2.wait_recv()
     u5 = cs2[9] + cb2[9]
@@ -398,7 +463,7 @@
     second = z - step32 * mapped
     out_o[4:6] = (second + over_tile(rz_new / rz_old) * z).reshape(2, 16, K)
 
-    for e in edges_k + edges_z + [core1, core2]:
+    for e in edges_k + edges_z + matrices + [core1, core2]:
         e.wait_send()
     for buf, slot in ((zb1, 0), (gb1, 2), (zb2, 3), (gb2, 5)):
         wait_bytes(buf, ssem.at[slot])
@@ -422,12 +487,17 @@
             pltpu.VMEM((10 * K, 2 * K), BF16),
             pltpu.VMEM((32, K), F32), pltpu.VMEM((2, 16, K), F32), pltpu.VMEM((32, K), F32),
             unit(4), unit(26), unit(8), unit(15, 8), unit(5), unit(5), unit(11), unit(11),
-            unit(4), unit(26), unit(9), unit(15, 9),
+            unit(4), unit(15, 4), unit(9), unit(15, 9),
             unit(2), unit(2), pltpu.VMEM((2, 8, K), F32), pltpu.VMEM((2, 8, K), F32),
             unit(2), unit(2), pltpu.VMEM((2, 8, K), F32), pltpu.VMEM((2, 8, K), F32),
+            pltpu.VMEM((2, 4 * K, K), F32), pltpu.VMEM((2, 4 * K, K), F32),
+            pltpu.VMEM((2, 4 * K, 2 * K), BF16),
+            pltpu.VMEM((2, 16, 4 * K), F32), pltpu.VMEM((2, 16, 4 * K), F32),
+            pltpu.VMEM((64, 4 * K), BF16),
             pltpu.SemaphoreType.DMA((12,)), pltpu.SemaphoreType.DMA((6,)),
             pltpu.SemaphoreType.DMA((6,)), pltpu.SemaphoreType.DMA((8,)),
-            pltpu.SemaphoreType.DMA((8,)),
+            pltpu.SemaphoreType.DMA((8,)), pltpu.SemaphoreType.DMA((4,)),
+            pltpu.SemaphoreType.DMA((4,)),
         ],
         compiler_params=pltpu.CompilerParams(
             collective_id=0, has_side_effects=True, vmem_limit_bytes=60 * 1024 * 1024

time: 52.5 us -> 49.9 us (0.950); the launches traced: 51.5 us -> 49.5 us
  Pallas kernels: 49.5 us -> 47.5 us
    pallas_call x1, Pallas kernels: 49.5 us -> 47.5 us  [on_device(): pl.pallas_call(kernel, name='pcg_step', out_shape=jax.ShapeDtypeStruct((6...]
where the time goes in v4:
time: 49.9 us; the launch traced here: 49.5 us
  Pallas kernels  47.5 us (95%)
  local copies, waits for them, and re-layouts  1.37 us (3%)
  between operations  0.64 us (1%)
    pallas_call x1, Pallas kernels, on_device(): pl.pallas_call(kernel, name='pcg_step', out_shape=jax.ShapeDtypeStruct((6...  47.5 us
    slice x1, local copies, waits for them, and re-layouts, on_device(): return (out[0:2], out[2:4], out[4:6])  1.37 us

profile of v4, /device:TPU:1, one launch (start us, length us, event | category | flops | bytes accessed | tf_op | source)
XLA Modules:
  0.0 49.5 jit_solution(470609248288691387)
XLA Ops:
  0.6 47.5 %pcg_step.1 = f32[6,16,128]{2,1,0:T(8,128)} custom-call(f32[2,16,128]{2,1,0:T(8,128)} %rs_h.1, f32[16,128]{1,0:T(8,128)} %cond_h.1, f32[4,4,128,128]{3,2,1,0:T(8,128)} %linv_h.1, f32[16,128,128]{2,1,0:T(8,128)} %basis_h.1, f32[1,1,128,128]{3,2,1,0:T(8,128)} %e0_h.1, f32[1,1,8,128,128]{4,3,2,1,0:T(8,128)} %nt_h.1, f32[1,1,128,128]{3,2,1,0:T(8,128)} %f0_h.1, ...), custom_call_target="tpu_custom_call" | custom-call | tf_op jit(solution)/shard_map/pcg_step/pallas_call | solution.py:475
  48.1 1.4 %fusion = (f32[2,16,128]{2,1,0:T(8,128)}, f32[2,16,128]{2,1,0:T(8,128)}, f32[2,16,128]{2,1,0:T(8,128)}) fusion(f32[6,16,128]{2,1,0:T(8,128)} %pcg_step.1), kind=kLoop, calls=%fused_computation | loop fusion | bytes 98304 | tf_op jit(solution)/shard_map/slice | solution.py:506

commit v5 on v4

--- a/solution.py
+++ b/solution.py
@@ -88,7 +88,7 @@
     pf, rf, basis2, linv2, pa, pb, ra, rb, gs, lb, wt, tmp,
     zs1, zb1, zs2, zb2, cs1, cb1, cs2, cb2, gs1, gb1, gs2, gb2,
     hrs, hrb, hcs, hcb, krs, krb, kcs, kcb,
-    hxs, hxb, hx2, hzs, hzb, hz2,
+    hxs, hxb, hx2, hzs, hzb, hz2, out,
     lsem, ssem, rsem, hsem, hrsem, msem, mrsem,
 ):
     X = lax.axis_index("gx")
@@ -434,13 +434,15 @@
     gs2[0] = gs2[0] + quadratic(u5 * (cs2[10] + cb2[10]))
     send_all(gs2, gb2, 5, g_peer)
     y = dot_w(jnp.concatenate([u0, u1, u2, u3, u4, u5], axis=1), gs[0 : 6 * K])
+    for e in edges_k + edges_z + matrices + [core1, core2]:
+        e.wait_send()
+    for buf, slot in ((zb1, 0), (gb1, 2), (zb2, 3)):
+        wait_bytes(buf, ssem.at[slot])
     wait_bytes(gb2, rsem.at[5])
     u9, q9 = products(gs2, gb2, 1, 5, 16)
     u8, q8 = products(gs2, gb2, 2, 6, 8)
     u7, q7 = products(gs2, gb2, 3, 7, 4)
     u6, q6 = products(gs2, gb2, 4, 8, 2)
-    y = y + dot_w(jnp.concatenate([u6, u7, u8, u9], axis=1), gs[6 * K : 10 * K])
-    mapped = near + spread_out(y)
     inner = all_sums(gs2, gb2, 0, 16)[0] + quadratic(q6 + q7 + q8 + q9)
 
     def over_lanes(t):
@@ -458,15 +460,20 @@
         )
 
     step32 = over_tile(step)
-    out_o[0:2] = (step32 * z).reshape(2, 16, K)
-    out_o[2:4] = (b32 - step32 * applied).reshape(2, 16, K)
+    out[0:2] = (step32 * z).reshape(2, 16, K)
+    out[2:4] = (b32 - step32 * applied).reshape(2, 16, K)
+    results = [pltpu.make_async_copy(out.at[pl.ds(0, 4)], out_o.at[pl.ds(0, 4)], lsem.at[0])]
+    results[0].start()
+    y = y + dot_w(jnp.concatenate([u6, u7, u8, u9], axis=1), gs[6 * K : 10 * K])
+    mapped = near + spread_out(y)
     second = z - step32 * mapped
-    out_o[4:6] = (second + over_tile(rz_new / rz_old) * z).reshape(2, 16, K)
-
-    for e in edges_k + edges_z + matrices + [core1, core2]:
-        e.wait_send()
-    for buf, slot in ((zb1, 0), (gb1, 2), (zb2, 3), (gb2, 5)):
-        wait_bytes(buf, ssem.at[slot])
+    out[4:6] = (second + over_tile(rz_new / rz_old) * z).reshape(2, 16, K)
+    results.append(pltpu.make_async_copy(out.at[pl.ds(4, 2)], out_o.at[pl.ds(4, 2)], lsem.at[1]))
+    results[1].start()
+
+    wait_bytes(gb2, ssem.at[5])
+    for part in results:
+        part.wait()
 
 
 def on_device(*args):
@@ -477,7 +484,7 @@
         name="pcg_step",
         out_shape=jax.ShapeDtypeStruct((6, 16, K), F32),
         in_specs=[pl.BlockSpec(memory_space=pl.ANY)] * 8,
-        out_specs=pl.BlockSpec(memory_space=pltpu.VMEM),
+        out_specs=pl.BlockSpec(memory_space=pl.ANY),
         scratch_shapes=[
             pltpu.VMEM((2, 16, K), F32), pltpu.VMEM((16, K), F32), square(4, 4), square(16),
             square(), square(8), square(), square(9),
@@ -493,7 +500,7 @@
             pltpu.VMEM((2, 4 * K, K), F32), pltpu.VMEM((2, 4 * K, K), F32),
             pltpu.VMEM((2, 4 * K, 2 * K), BF16),
             pltpu.VMEM((2, 16, 4 * K), F32), pltpu.VMEM((2, 16, 4 * K), F32),
-            pltpu.VMEM((64, 4 * K), BF16),
+            pltpu.VMEM((64, 4 * K), BF16), pltpu.VMEM((6, 16, K), F32),
             pltpu.SemaphoreType.DMA((12,)), pltpu.SemaphoreType.DMA((6,)),
             pltpu.SemaphoreType.DMA((6,)), pltpu.SemaphoreType.DMA((8,)),
             pltpu.SemaphoreType.DMA((8,)), pltpu.SemaphoreType.DMA((4,)),

time: 49.9 us -> 49.8 us (level)
  no operation moved by 1% of the time
where the time goes in v5:
time: 49.8 us; the launch traced here: 49.4 us
  Pallas kernels  47.4 us (95%)
  local copies, waits for them, and re-layouts  1.37 us (3%)
  between operations  0.64 us (1%)
    pallas_call x1, Pallas kernels, on_device(): pl.pallas_call(kernel, name='pcg_step', out_shape=jax.ShapeDtypeStruct((6...  47.4 us
    slice x1, local copies, waits for them, and re-layouts, on_device(): return (out[0:2], out[2:4], out[4:6])  1.37 us

profile of v5, /device:TPU:1, one launch (start us, length us, event | category | flops | bytes accessed | tf_op | source)
XLA Modules:
  0.0 49.4 jit_solution(14168579173628564281)
XLA Ops:
  0.6 47.4 %pcg_step.1 = f32[6,16,128]{2,1,0:T(8,128)} custom-call(f32[2,16,128]{2,1,0:T(8,128)} %rs_h.1, f32[16,128]{1,0:T(8,128)} %cond_h.1, f32[4,4,128,128]{3,2,1,0:T(8,128)} %linv_h.1, f32[16,128,128]{2,1,0:T(8,128)} %basis_h.1, f32[1,1,128,128]{3,2,1,0:T(8,128)} %e0_h.1, f32[1,1,8,128,128]{4,3,2,1,0:T(8,128)} %nt_h.1, f32[1,1,128,128]{3,2,1,0:T(8,128)} %f0_h.1, ...), custom_call_target="tpu_custom_call" | custom-call | tf_op jit(solution)/shard_map/pcg_step/pallas_call | solution.py:482
  48.1 1.4 %fusion = (f32[2,16,128]{2,1,0:T(8,128)}, f32[2,16,128]{2,1,0:T(8,128)}, f32[2,16,128]{2,1,0:T(8,128)}) fusion(f32[6,16,128]{2,1,0:T(8,128)} %pcg_step.1), kind=kLoop, calls=%fused_computation | loop fusion | bytes 98304 | tf_op jit(solution)/shard_map/slice | solution.py:513

commit v6 on v4

--- a/solution.py
+++ b/solution.py
@@ -86,7 +86,7 @@
     out_o,
     rs, cond, linv, basis, e0, nt, f0, nf,
     pf, rf, basis2, linv2, pa, pb, ra, rb, gs, lb, wt, tmp,
-    zs1, zb1, zs2, zb2, cs1, cb1, cs2, cb2, gs1, gb1, gs2, gb2,
+    zs1, zb1, zs2, zb2, zx2, cs1, cb1, cs2, cb2, gs1, gb1, gs2, gb2,
     hrs, hrb, hcs, hcb, krs, krb, kcs, kcb,
     hxs, hxb, hx2, hzs, hzb, hz2,
     lsem, ssem, rsem, hsem, hrsem, msem, mrsem,
@@ -406,22 +406,30 @@
     u0 = coefficients(wt)
     put(zs2, dot_w(u0, pa[...]), 1)
     low = dot_w(u0, pb[...])
-    put(zs2, low[:, 0 : 3 * K], 5)
+    put(zs2, low[:, 0 : 2 * K], 5)
+    m1, image1 = zs2[4], low[:, 2 * K : 3 * K]
+    zs2[4] = jnp.where(Z % 2 == 0, m1, image1)
+    zs2[7] = m1
     near = leaf_apply(applied)
     inner = jnp.concatenate([columns(b32 * z), columns(z * applied)], axis=0)
     inner = inner + pltpu.roll(inner, 64, 1)
     inner = inner + pltpu.roll(inner, 32, 1)
     zs2[0] = jnp.where(lane2 < 32, inner[0:2], jnp.where(lane2 < 64, inner[2:4], 0.0)) + quadratic(
-        columns(applied * near) + u0 * low[:, 3 * K :]
-    )
-    send_all(zs2, zb2, 3, z_peer)
+        columns(applied * near) + u0 * low[:, 3 * K :] + m1 * image1
+    )
+    for d in ORDER:
+        send(zs2.at[pl.ds(0, 7)], zb2.at[d - 1], ssem.at[3], rsem.at[3], z_peer(d))
+    pair = send(zs2.at[pl.ds(7, 1)], zx2, ssem.at[6], rsem.at[6], z_peer(1))
     wait_bytes(zb2, rsem.at[3])
     u4 = all_sums(zs2, zb2, 1, 16)[0]
     up = dot_w(u4, ra[...])
     mapped_up = dot_w(u4, rb[...])
     u3, q3 = products(zs2, zb2, 2, 5, 8)
     u2, q2 = products(zs2, zb2, 3, 6, 4)
-    u1, q1 = products(zs2, zb2, 4, 7, 2)
+    pair.wait_recv()
+    u1 = zs2[7] + zx2[0]
+    terms = [zs2[4]] + [zb2[d, 4] for d in range(15)]
+    q1 = 2.0 * butterfly([terms[i] * terms[i + 1] for i in range(0, 16, 2)])
     cs2[0] = all_sums(zs2, zb2, 0, 16)[0] + quadratic(q1 + q2 + q3 + u4 * mapped_up[:, 5 * K :])
     put(cs2, up[:, 0 : 4 * K], 1)
     put(cs2, mapped_up[:, 0 : 4 * K], 5)
@@ -463,7 +471,7 @@
     second = z - step32 * mapped
     out_o[4:6] = (second + over_tile(rz_new / rz_old) * z).reshape(2, 16, K)
 
-    for e in edges_k + edges_z + matrices + [core1, core2]:
+    for e in edges_k + edges_z + matrices + [core1, core2, pair]:
         e.wait_send()
     for buf, slot in ((zb1, 0), (gb1, 2), (zb2, 3), (gb2, 5)):
         wait_bytes(buf, ssem.at[slot])
@@ -486,7 +494,7 @@
             pltpu.VMEM((K, 10 * K), BF16), pltpu.VMEM((K, 12 * K), BF16),
             pltpu.VMEM((10 * K, 2 * K), BF16),
             pltpu.VMEM((32, K), F32), pltpu.VMEM((2, 16, K), F32), pltpu.VMEM((32, K), F32),
-            unit(4), unit(26), unit(8), unit(15, 8), unit(5), unit(5), unit(11), unit(11),
+            unit(4), unit(26), unit(8), unit(15, 7), unit(1), unit(5), unit(5), unit(11), unit(11),
             unit(4), unit(15, 4), unit(9), unit(15, 9),
             unit(2), unit(2), pltpu.VMEM((2, 8, K), F32), pltpu.VMEM((2, 8, K), F32),
             unit(2), unit(2), pltpu.VMEM((2, 8, K), F32), pltpu.VMEM((2, 8, K), F32),
@@ -494,8 +502,8 @@
             pltpu.VMEM((2, 4 * K, 2 * K), BF16),
             pltpu.VMEM((2, 16, 4 * K), F32), pltpu.VMEM((2, 16, 4 * K), F32),
             pltpu.VMEM((64, 4 * K), BF16),
-            pltpu.SemaphoreType.DMA((12,)), pltpu.SemaphoreType.DMA((6,)),
-            pltpu.SemaphoreType.DMA((6,)), pltpu.SemaphoreType.DMA((8,)),
+            pltpu.SemaphoreType.DMA((12,)), pltpu.SemaphoreType.DMA((7,)),
+            pltpu.SemaphoreType.DMA((7,)), pltpu.SemaphoreType.DMA((8,)),
             pltpu.SemaphoreType.DMA((8,)), pltpu.SemaphoreType.DMA((4,)),
             pltpu.SemaphoreType.DMA((4,)),
         ],

time: 49.9 us -> 49.5 us (level)
  no operation moved by 1% of the time
where the time goes in v6:
time: 49.5 us; the launch traced here: 49.3 us
  Pallas kernels  47.3 us (96%)
  local copies, waits for them, and re-layouts  1.37 us (3%)
  between operations  0.64 us (1%)
    pallas_call x1, Pallas kernels, on_device(): pl.pallas_call(kernel, name='pcg_step', out_shape=jax.ShapeDtypeStruct((6...  47.3 us
    slice x1, local copies, waits for them, and re-layouts, on_device(): return (out[0:2], out[2:4], out[4:6])  1.37 us

profile of v6, /device:TPU:1, one launch (start us, length us, event | category | flops | bytes accessed | tf_op | source)
XLA Modules:
  0.0 49.3 jit_solution(7141512503875826220)
XLA Ops:
  0.6 47.3 %pcg_step.1 = f32[6,16,128]{2,1,0:T(8,128)} custom-call(f32[2,16,128]{2,1,0:T(8,128)} %rs_h.1, f32[16,128]{1,0:T(8,128)} %cond_h.1, f32[4,4,128,128]{3,2,1,0:T(8,128)} %linv_h.1, f32[16,128,128]{2,1,0:T(8,128)} %basis_h.1, f32[1,1,128,128]{3,2,1,0:T(8,128)} %e0_h.1, f32[1,1,8,128,128]{4,3,2,1,0:T(8,128)} %nt_h.1, f32[1,1,128,128]{3,2,1,0:T(8,128)} %f0_h.1, ...), custom_call_target="tpu_custom_call" | custom-call | tf_op jit(solution)/shard_map/pcg_step/pallas_call | solution.py:483
  47.9 1.4 %fusion = (f32[2,16,128]{2,1,0:T(8,128)}, f32[2,16,128]{2,1,0:T(8,128)}, f32[2,16,128]{2,1,0:T(8,128)}) fusion(f32[6,16,128]{2,1,0:T(8,128)} %pcg_step.1), kind=kLoop, calls=%fused_computation | loop fusion | bytes 98304 | tf_op jit(solution)/shard_map/slice | solution.py:514
